TPU v7x, 32 devices: a whole 2x2x4 slice. The times are simulated.
32 devices in a mesh: slab: 8 (over z, core), deal: 4 (over y, x).
Axes of the slice: x: 2, y: 2, z: 4, core: 2. Of those that a mesh axis runs over, the one named last changes fastest.
Arguments:
- offsets: float32 [32768, 3, 128], P(('slab', 'deal')), may hold values from -0.5 to 0.5
- velocity: float32 [32768, 3, 128], P(('slab', 'deal')), may hold values from -6 to 6
- affine: float32 [32768, 9, 128], P(('slab', 'deal')), may hold values from -6 to 6
- particle_mass: float32 [32768, 128], P(('slab', 'deal')), may hold values from 0.5 to 2
- cell_in_tile: int32 [32768, 128], P(('slab', 'deal')), may hold values from 0 to 255
- block_tile: int32 [32768], P(('slab', 'deal')), may hold values from 0 to 2047, as said below
- live_blocks: int32 [8, 4], P('slab', 'deal'), may hold values from 512 to 1024, as said below
- send_lists: int32 [8, 4, 2, 16], P('slab', 'deal'), may hold values from 0 to 1023, as said below
- send_counts: int32 [8, 4, 2], P('slab', 'deal'), may hold values from 0 to 16, as said below
Outputs:
- updated_particles: float32 [32768, 15, 128], P(('slab', 'deal'))
- arrivals: float32 [8, 4, 2, 16, 16, 128], P('slab', 'deal')
- grid_velocity: float32 [3, 512, 8192], P(None, 'slab', 'deal')
Inputs may be any that keep to these rules, and one draw needn't show every extreme that they name: `block_tile`: blocks are sorted by cell: on device (s, d) the tiles never fall along its blocks and lie in [max(d * R - M, 0), min((d + 1) * R + M, 2048)) with R = 512 and M = max(R // 16, 1); some device with d > 0 reaches d * R - M. `live_blocks`: some device has all 1024 blocks live. `send_lists`: the 32 entries of one device's two lists are distinct blocks of that device. `send_counts`: counts toward a slab beyond the ends are zero; some device sends 16 blocks downslope.
All inputs are finite; a program needn't handle non-finite values.
Results may differ from a plain program's by a relative error of at most 0.000073.
Values sent between devices are 32-bit elements; how exact they have to be, the bound alone decides.
A program may use at most 128 MiB of HBM per device.

v0:
```python
import math

import jax
import jax.numpy as jnp
from jax import lax
from jax.sharding import PartitionSpec as P

PX = 64
PLANE = 8192
TILE = 256


time_step = 0.1
viscosity = 0.2
gravity_pull = (3.0, 0.0, -5.0)


def extended(x, sides, width):
    for axis, dim in sides:
        count, length = (lax.axis_size(axis), x.shape[dim])
        up = [(i, (i + 1) % count) for i in range(count - 1)]
        down = [(j, i) for i, j in up]
        last = lax.slice_in_dim(x, length - width, length, axis=dim)
        initial = lax.slice_in_dim(x, 0, width, axis=dim)
        before = lax.ppermute(last, axis, up)
        after = lax.ppermute(initial, axis, down)
        x = jnp.concatenate([before, x, after], axis=dim)
    return x


def from_behind(x, axis, by):
    count = lax.axis_size(axis)
    pairs = [(i, i + by) for i in range(count) if 0 <= i + by < count]
    return lax.ppermute(x, axis, pairs)


def momentum(offsets, velocity, affine):
    columns = []
    for column in range(3):
        total = velocity[:, column]
        for inner in range(3):
            total = total - affine[:, 3 * column + inner] * offsets[:, inner]
        columns.append(total)
    return jnp.stack(columns, axis=1)


def grid_update(summed):
    floor_mass = jnp.maximum(summed[0], 1.0)
    speeds = []
    for column in range(3):
        speeds.append(summed[1 + column] / floor_mass + time_step * gravity_pull[column])
    return jnp.stack(speeds, axis=0)


def smooth_planes(speed):
    padded = extended(speed, (("slab", 1),), 1)
    return speed + viscosity * (padded[:, 2:] + padded[:, :-2] - 2.0 * speed)


def new_state(offsets, moved):
    shifted = offsets + time_step * moved
    affine_rows = []
    for column in range(3):
        for inner in range(3):
            affine_rows.append(-4.0 * moved[:, column] * offsets[:, inner])
    return jnp.concatenate([shifted, moved, jnp.stack(affine_rows, axis=1)], axis=1)


def body(
    offsets,
    velocity,
    affine,
    particle_mass,
    cell_in_tile,
    block_tile,
    live_blocks,
    send_lists,
    send_counts,
):
    highest = lax.Precision.HIGHEST
    blocks_here = offsets.shape[0]
    tile_count = PX * PLANE // TILE
    active = (jnp.arange(blocks_here, dtype=jnp.int32) < live_blocks[0, 0]).astype(jnp.float32)
    weight = particle_mass * active[:, None]
    moment = momentum(offsets, velocity, affine)
    deposit = jnp.concatenate([weight[:, None, :], weight[:, None, :] * moment], axis=1)
    group_size = math.gcd(blocks_here, 128)
    group_count = blocks_here // group_size
    grouped_deposit = deposit.reshape(group_count, group_size, 4, 128)
    grouped_cells = cell_in_tile.reshape(group_count, group_size, 128)
    grouped_tiles = block_tile.reshape(group_count, group_size)
    tile_slots = jnp.arange(TILE, dtype=jnp.int32)
    tile_labels = jnp.arange(tile_count, dtype=jnp.int32)

    def scatter_group(accumulated, pieces):
        part_deposit, part_cells, part_tiles = pieces
        selector = (part_cells[:, :, None] == tile_slots).astype(jnp.float32)
        per_block = jnp.einsum("bcp,bpk->bck", part_deposit, selector, precision=highest)
        placing = (part_tiles[:, None] == tile_labels).astype(jnp.float32)
        return (
            accumulated + jnp.einsum("bt,bck->ctk", placing, per_block, precision=highest),
            None,
        )

    start_grid = jnp.zeros((4, tile_count, TILE), jnp.float32)
    accumulated, unused = lax.scan(
        scatter_group, start_grid, (grouped_deposit, grouped_cells, grouped_tiles)
    )
    partial_grid = accumulated.reshape(4, PX, PLANE)
    summed = lax.psum_scatter(partial_grid, "deal", scatter_dimension=2, tiled=True)
    own_share = smooth_planes(grid_update(summed))
    settled = lax.all_gather(own_share, "deal", axis=2, tiled=True)
    tiles_view = settled.reshape(3, tile_count, TILE)

    def gather_group(pieces):
        part_cells, part_tiles = pieces
        selector = (part_cells[:, :, None] == tile_slots).astype(jnp.float32)
        chosen = jnp.take(tiles_view, part_tiles, axis=1)
        return jnp.einsum("cbk,bpk->bcp", chosen, selector, precision=highest)

    moved = lax.map(gather_group, (grouped_cells, grouped_tiles)).reshape(blocks_here, 3, 128)
    state = new_state(offsets, moved)
    records = jnp.concatenate([state, particle_mass[:, None, :]], axis=1)
    lists_here = send_lists[0, 0]
    counts_here = send_counts[0, 0]
    mig_slots = lists_here.shape[1]
    leaving = records[lists_here]
    keeping = (jnp.arange(mig_slots, dtype=jnp.int32)[None, :] < counts_here[:, None]).astype(
        jnp.float32
    )
    leaving = leaving * keeping[:, :, None, None]
    from_left = from_behind(leaving[0], "slab", 1)
    from_right = from_behind(leaving[1], "slab", -1)
    arrivals = jnp.stack([from_left, from_right], axis=0)[None, None]
    return (state, arrivals, own_share)


def solution(mesh):
    placed = (
        P(("slab", "deal"), None, None),
        P(("slab", "deal"), None, None),
        P(("slab", "deal"), None, None),
        P(("slab", "deal"), None),
        P(("slab", "deal"), None),
        P(("slab", "deal")),
        P("slab", "deal"),
        P("slab", "deal", None, None),
        P("slab", "deal", None),
    )
    return jax.shard_map(
        body,
        mesh=mesh,
        in_specs=placed,
        out_specs=(
            P(("slab", "deal"), None, None),
            P("slab", "deal", None, None, None, None),
            P(None, "slab", "deal"),
        ),
        check_vma=False,
    )
```

profile of v0, /device:TPU:1, one launch (start us, length us, event | category | flops | bytes accessed | tf_op | source)
XLA Modules:
  0.0 518.5 jit_solution(13218201500276755458)
XLA Ops:
  18.7 129.0 %while.23 = (s32[]{:T(128)}, f32[4,2048,256]{1,2,0:T(8,128)}, f32[8,128,4,128]{3,2,1,0:T(4,128)}, s32[8,128,128]{2,1,0:T(8,128)}, s32[8,128]{1,0:T(8,128)}, /*index=5*/s32[]{:T(128)}, s32[]{:T(128)}) while((s32[]{:T(128)}, f32[4,2048,256]{1,2,0:T(8,128)}, f32[8,128,4,128]{3,2,1,0:T(4,128)}, s32[8,128,128]{2,1,0:T(8,128)}, ...), condition=%wide.region_1.2_spmd.clone, body=%wide.region_0.1_spmd.clone.sunk | while | flops 3431202816 | bytes 18286684 | solution.py:106
  40.9 8.4 %bitcast_add_fusion.2 = f32[4,2048,256]{1,2,0:T(8,128)} fusion(f32[4,2048,256]{1,2,0:T(8,128)} %get-tuple-element.234, pred[]{:T(512)S(6)} %compare.3, f32[128,4,256]{2,1,0:T(4,128)S(1)} %fusion.76, s32[128]{0:T(128)S(1)} %fusion.77), kind=kOutput, calls=%fused_computation.24.clone.1 | convolution fusion | flops 3225681920 | bytes 17302016 | tf_op jit(solution)/shard_map/while/body/eval_jaxpr/bt,bck->ctk/dot_general | solution.py:101
  57.3 8.4 %bitcast_add_fusion.2 = f32[4,2048,256]{1,2,0:T(8,128)} fusion(f32[4,2048,256]{1,2,0:T(8,128)} %get-tuple-element.234, pred[]{:T(512)S(6)} %compare.3, f32[128,4,256]{2,1,0:T(4,128)S(1)} %fusion.76, s32[128]{0:T(128)S(1)} %fusion.77), kind=kOutput, calls=%fused_computation.24.clone.1 | convolution fusion | flops 3225681920 | bytes 17302016 | tf_op jit(solution)/shard_map/while/body/eval_jaxpr/bt,bck->ctk/dot_general | solution.py:101
  73.7 8.4 %bitcast_add_fusion.2 = f32[4,2048,256]{1,2,0:T(8,128)} fusion(f32[4,2048,256]{1,2,0:T(8,128)} %get-tuple-element.234, pred[]{:T(512)S(6)} %compare.3, f32[128,4,256]{2,1,0:T(4,128)S(1)} %fusion.76, s32[128]{0:T(128)S(1)} %fusion.77), kind=kOutput, calls=%fused_computation.24.clone.1 | convolution fusion | flops 3225681920 | bytes 17302016 | tf_op jit(solution)/shard_map/while/body/eval_jaxpr/bt,bck->ctk/dot_general | solution.py:101
  90.1 8.4 %bitcast_add_fusion.2 = f32[4,2048,256]{1,2,0:T(8,128)} fusion(f32[4,2048,256]{1,2,0:T(8,128)} %get-tuple-element.234, pred[]{:T(512)S(6)} %compare.3, f32[128,4,256]{2,1,0:T(4,128)S(1)} %fusion.76, s32[128]{0:T(128)S(1)} %fusion.77), kind=kOutput, calls=%fused_computation.24.clone.1 | convolution fusion | flops 3225681920 | bytes 17302016 | tf_op jit(solution)/shard_map/while/body/eval_jaxpr/bt,bck->ctk/dot_general | solution.py:101
  106.5 8.4 %bitcast_add_fusion.2 = f32[4,2048,256]{1,2,0:T(8,128)} fusion(f32[4,2048,256]{1,2,0:T(8,128)} %get-tuple-element.234, pred[]{:T(512)S(6)} %compare.3, f32[128,4,256]{2,1,0:T(4,128)S(1)} %fusion.76, s32[128]{0:T(128)S(1)} %fusion.77), kind=kOutput, calls=%fused_computation.24.clone.1 | convolution fusion | flops 3225681920 | bytes 17302016 | tf_op jit(solution)/shard_map/while/body/eval_jaxpr/bt,bck->ctk/dot_general | solution.py:101
  122.9 8.4 %bitcast_add_fusion.2 = f32[4,2048,256]{1,2,0:T(8,128)} fusion(f32[4,2048,256]{1,2,0:T(8,128)} %get-tuple-element.234, pred[]{:T(512)S(6)} %compare.3, f32[128,4,256]{2,1,0:T(4,128)S(1)} %fusion.76, s32[128]{0:T(128)S(1)} %fusion.77), kind=kOutput, calls=%fused_computation.24.clone.1 | convolution fusion | flops 3225681920 | bytes 17302016 | tf_op jit(solution)/shard_map/while/body/eval_jaxpr/bt,bck->ctk/dot_general | solution.py:101
  139.3 8.4 %bitcast_add_fusion.2 = f32[4,2048,256]{1,2,0:T(8,128)} fusion(f32[4,2048,256]{1,2,0:T(8,128)} %get-tuple-element.234, pred[]{:T(512)S(6)} %compare.3, f32[128,4,256]{2,1,0:T(4,128)S(1)} %fusion.76, s32[128]{0:T(128)S(1)} %fusion.77), kind=kOutput, calls=%fused_computation.24.clone.1 | convolution fusion | flops 3225681920 | bytes 17302016 | tf_op jit(solution)/shard_map/while/body/eval_jaxpr/bt,bck->ctk/dot_general | solution.py:101
  147.7 8.7 %copy.45 = f32[4,2048,256]{2,1,0:T(8,128)} copy(f32[4,2048,256]{1,2,0:T(8,128)} %get-tuple-element.72) | data formatting | bytes 16777216 | tf_op jit(solution)/shard_map/while | solution.py:106
  156.4 9.5 %reshape.134 = f32[4,64,8192]{2,1,0:T(8,128)} reshape(f32[4,2048,256]{2,1,0:T(8,128)} %copy.45) | data formatting | bytes 16777216 | tf_op jit(solution)/shard_map/reshape | solution.py:109
  165.9 88.5 %reduce-scatter.2.cloned.1.call-done = f32[4,64,2048]{2,1,0:T(8,128)} async-done(((f32[4,64,8192]{2,1,0:T(8,128)}), f32[4,64,2048]{2,1,0:T(8,128)}) %reduce-scatter.2.cloned.1.call-update) | async-done | bytes 2097168 | tf_op jit(solution)/shard_map/reduce_scatter | solution.py:110
  264.8 70.6 %all-gather.2.cloned.1.call-done = f32[3,64,8192]{2,1,0:T(8,128)} async-done(((f32[3,64,2048]{2,1,0:T(8,128)}), f32[3,64,8192]{2,1,0:T(8,128)}) %all-gather.2.cloned.1.call-update) | async-done | bytes 6291472 | tf_op jit(solution)/shard_map/all_gather | solution.py:112
  335.5 7.1 %reshape.135 = f32[3,2048,256]{2,1,0:T(8,128)} reshape(f32[3,64,8192]{2,1,0:T(8,128)} %all-gather.2.cloned.1.call-done) | data formatting | bytes 12582912 | tf_op jit(solution)/shard_map/reshape | solution.py:113
  342.5 10.7 %copy.46 = f32[3,2048,256]{2,0,1:T(4,128)} copy(f32[3,2048,256]{2,1,0:T(8,128)} %reshape.135) | data formatting | bytes 12582912
  353.3 130.0 %while.22 = (s32[]{:T(128)}, f32[8,128,3,128]{3,1,0,2:T(8,128)S(1)}, s32[8,128]{1,0:T(8,128)}, f32[3,2048,256]{2,0,1:T(4,128)}, s32[8,128,128]{2,1,0:T(8,128)}, /*index=5*/s32[]{:T(128)}) while((s32[]{:T(128)}, f32[8,128,3,128]{3,1,0,2:T(8,128)S(1)}, s32[8,128]{1,0:T(8,128)}, f32[3,2048,256]{2,0,1:T(4,128)}, ...), condition=%wide.region_4.5_spmd.clone, body=%wide.region_3.4_spmd.clone.sunk | while | flops 155289728 | bytes 2038613 | solution.py:121
  360.5 8.9 %fusion.72 = f32[1,128,3,128]{3,2,1,0:T(4,128)S(1)} fusion(s32[128,128]{1,0:T(8,128)S(1)} %dynamic-slice_bitcast_fusion.4, f32[128,3,256]{2,1,0:T(4,128)} %gather_fusion, pred[128]{0:T(512)(128)(4,1)S(1)} %compare_and_fusion.2), kind=kOutput, calls=%fused_computation.8.clone.1 | convolution fusion | flops 155287552 | bytes 655488 | tf_op jit(solution)/shard_map/while/body/eval_jaxpr/cbk,bpk->bcp/dot_general | solution.py:119
  376.8 8.9 %fusion.72 = f32[1,128,3,128]{3,2,1,0:T(4,128)S(1)} fusion(s32[128,128]{1,0:T(8,128)S(1)} %dynamic-slice_bitcast_fusion.4, f32[128,3,256]{2,1,0:T(4,128)} %gather_fusion, pred[128]{0:T(512)(128)(4,1)S(1)} %compare_and_fusion.2), kind=kOutput, calls=%fused_computation.8.clone.1 | convolution fusion | flops 155287552 | bytes 655488 | tf_op jit(solution)/shard_map/while/body/eval_jaxpr/cbk,bpk->bcp/dot_general | solution.py:119
  393.1 8.9 %fusion.72 = f32[1,128,3,128]{3,2,1,0:T(4,128)S(1)} fusion(s32[128,128]{1,0:T(8,128)S(1)} %dynamic-slice_bitcast_fusion.4, f32[128,3,256]{2,1,0:T(4,128)} %gather_fusion, pred[128]{0:T(512)(128)(4,1)S(1)} %compare_and_fusion.2), kind=kOutput, calls=%fused_computation.8.clone.1 | convolution fusion | flops 155287552 | bytes 655488 | tf_op jit(solution)/shard_map/while/body/eval_jaxpr/cbk,bpk->bcp/dot_general | solution.py:119
  409.3 8.9 %fusion.72 = f32[1,128,3,128]{3,2,1,0:T(4,128)S(1)} fusion(s32[128,128]{1,0:T(8,128)S(1)} %dynamic-slice_bitcast_fusion.4, f32[128,3,256]{2,1,0:T(4,128)} %gather_fusion, pred[128]{0:T(512)(128)(4,1)S(1)} %compare_and_fusion.2), kind=kOutput, calls=%fused_computation.8.clone.1 | convolution fusion | flops 155287552 | bytes 655488 | tf_op jit(solution)/shard_map/while/body/eval_jaxpr/cbk,bpk->bcp/dot_general | solution.py:119
  425.6 8.9 %fusion.72 = f32[1,128,3,128]{3,2,1,0:T(4,128)S(1)} fusion(s32[128,128]{1,0:T(8,128)S(1)} %dynamic-slice_bitcast_fusion.4, f32[128,3,256]{2,1,0:T(4,128)} %gather_fusion, pred[128]{0:T(512)(128)(4,1)S(1)} %compare_and_fusion.2), kind=kOutput, calls=%fused_computation.8.clone.1 | convolution fusion | flops 155287552 | bytes 655488 | tf_op jit(solution)/shard_map/while/body/eval_jaxpr/cbk,bpk->bcp/dot_general | solution.py:119
  441.8 8.9 %fusion.72 = f32[1,128,3,128]{3,2,1,0:T(4,128)S(1)} fusion(s32[128,128]{1,0:T(8,128)S(1)} %dynamic-slice_bitcast_fusion.4, f32[128,3,256]{2,1,0:T(4,128)} %gather_fusion, pred[128]{0:T(512)(128)(4,1)S(1)} %compare_and_fusion.2), kind=kOutput, calls=%fused_computation.8.clone.1 | convolution fusion | flops 155287552 | bytes 655488 | tf_op jit(solution)/shard_map/while/body/eval_jaxpr/cbk,bpk->bcp/dot_general | solution.py:119
  458.1 8.9 %fusion.72 = f32[1,128,3,128]{3,2,1,0:T(4,128)S(1)} fusion(s32[128,128]{1,0:T(8,128)S(1)} %dynamic-slice_bitcast_fusion.4, f32[128,3,256]{2,1,0:T(4,128)} %gather_fusion, pred[128]{0:T(512)(128)(4,1)S(1)} %compare_and_fusion.2), kind=kOutput, calls=%fused_computation.8.clone.1 | convolution fusion | flops 155287552 | bytes 655488 | tf_op jit(solution)/shard_map/while/body/eval_jaxpr/cbk,bpk->bcp/dot_general | solution.py:119
  474.3 8.9 %fusion.72 = f32[1,128,3,128]{3,2,1,0:T(4,128)S(1)} fusion(s32[128,128]{1,0:T(8,128)S(1)} %dynamic-slice_bitcast_fusion.4, f32[128,3,256]{2,1,0:T(4,128)} %gather_fusion, pred[128]{0:T(512)(128)(4,1)S(1)} %compare_and_fusion.2), kind=kOutput, calls=%fused_computation.8.clone.1 | convolution fusion | flops 155287552 | bytes 655488 | tf_op jit(solution)/shard_map/while/body/eval_jaxpr/cbk,bpk->bcp/dot_general | solution.py:119
  488.8 8.1 %copy.48 = f32[1024,16,128]{2,1,0:T(8,128)} copy(f32[1024,16,128]{2,0,1:T(8,128)S(1)} %get-tuple-element.162) | data formatting | bytes 16777216 | tf_op jit(solution)/shard_map/concatenate | solution.py:123
  (133 shorter events, 170.2 us)
Async XLA Ops:
  7.2 3.1 copy-start
  7.2 247.3 %reduce-scatter.2.cloned.1.call-start = ((), (), s32[]{:S(2)}) async-start(), calls=%async_computation.1 | async-start | bytes 10485760 | tf_op jit(solution)/shard_map/reduce_scatter | solution.py:110
  10.3 3.2 copy-start.1
  165.8 169.6 %all-gather.2.cloned.1.call-start = ((), (), s32[]{:S(2)}) async-start(), calls=%async_computation.2 | async-start | bytes 7864320 | tf_op jit(solution)/shard_map/all_gather | solution.py:112
  256.3 5.9 %collective-permute-start = (f32[3,1,2048]{2,1,0:T(1,128)S(1)}, f32[3,1,2048]{2,1,0:T(1,128)S(1)}, u32[]{:S(2)}, u32[]{:S(2)}) collective-permute-start(f32[3,1,2048]{2,1,0:T(1,128)S(1)} %get-tuple-element.158), channel_id=1, source_target_pairs={{4,0},{8,4},{12,8},{16,12},{20,16},{24,20},{28,24},{5,1},{9,5},{13... | collective-permute-start | bytes 73736 | tf_op jit(solution)/shard_map/ppermute | solution.py:26
  259.0 5.7 %copy-start.4 = (s32[1,1,2,16]{3,2,1,0:T(2,128)S(1)}, s32[1,1,2,16]{3,2,1,0:T(2,128)}, u32[]{:S(2)}) copy-start(s32[1,1,2,16]{3,2,1,0:T(2,128)} %param.20) | copy-start | bytes 388
  259.0 5.8 %copy-start.5 = (s32[1,1,2]{2,1,0:T(1,128)S(1)}, s32[1,1,2]{2,1,0:T(1,128)}, u32[]{:S(2)}) copy-start(s32[1,1,2]{2,1,0:T(1,128)} %param.21) | copy-start | bytes 28
  259.0 3.9 collective-permute-start.1
  484.4 1.0 copy-start.2
  485.6 3.2 copy-start.3
  501.0 9.0 %collective-permute-start.2 = (f32[16,16,128]{2,1,0:T(8,128)S(1)}, f32[16,16,128]{2,1,0:T(8,128)S(1)}, u32[]{:S(2)}, u32[]{:S(2)}) collective-permute-start(f32[16,16,128]{2,1,0:T(8,128)S(1)} %get-tuple-element.160), channel_id=1, source_target_pairs={{0,4},{4,8},{8,12},{12,16},{16,20},{20,24},{24,28},{1,5},{5,9},{9,... | collective-permute-start | bytes 393224 | tf_op jit(solution)/shard_map/ppermute | solution.py:34
  504.7 6.3 %collective-permute-start.3 = (f32[16,16,128]{2,1,0:T(8,128)S(1)}, f32[16,16,128]{2,1,0:T(8,128)S(1)}, u32[]{:S(2)}, u32[]{:S(2)}) collective-permute-start(f32[16,16,128]{2,1,0:T(8,128)S(1)} %get-tuple-element.161), channel_id=1, source_target_pairs={{4,0},{8,4},{12,8},{16,12},{20,16},{24,20},{28,24},{5,1},{9,5},{13... | collective-permute-start | bytes 393224 | tf_op jit(solution)/shard_map/ppermute | solution.py:34
Sparse Core Ops, SparseCore 0:
  166.0 88.4 reduce-scatter.1
  264.8 70.6 all-gather.1
where the time goes:
time: 522 us; the launch traced here: 519 us
  matrix products  188 us (36%)
  waiting for transfers between devices  161 us (31%)
  local copies, waits for them, and re-layouts  112 us (21%)
  other arithmetic  30.7 us (6%)
  between operations  15 us (3%)
  starting transfers between devices  11.5 us (2%)
    reduce_scatter x1, waiting for transfers between devices, body(): lax.psum_scatter(partial_grid, 'deal', scatter_dimension=2, tiled=True)  88.5 us
    dot_general x8, matrix products, gather_group(): return jnp.einsum('cbk,bpk->bcp', chosen, selector, precision=highest)  71.3 us
    all_gather x1, waiting for transfers between devices, body(): settled = lax.all_gather(own_share, 'deal', axis=2, tiled=True)  70.6 us
    dot_general x8, matrix products, scatter_group(): jnp.einsum('bt,bck->ctk', placing, per_block, precision=highest)  64.7 us
    dot_general x8, matrix products, scatter_group(): jnp.einsum('bcp,bpk->bck', part_deposit, selector, precision=highest)  51.9 us
    gather x8, local copies, waits for them, and re-layouts, gather_group(): chosen = jnp.take(tiles_view, part_tiles, axis=1)  40.3 us
    unnamed x14, local copies, waits for them, and re-layouts  15.2 us
  transfers between devices with their start and end apart: 6, of which 4 were waited for; matrix products, arithmetic and copies ran while one was open for 1% of the time, Pallas kernels for 0%

commit v1 on v0

v1 whole, which is shorter than its diff:
```python
import functools

import jax
import jax.numpy as jnp
from jax import lax
from jax.experimental import pallas as pl
from jax.experimental.pallas import tpu as pltpu
from jax.sharding import PartitionSpec as P

PX = 64
PLANE = 8192
TILE = 256
LANES = 128

time_step = 0.1
viscosity = 0.2
gravity_pull = (3.0, 0.0, -5.0)

VMEM_LIMIT = 40 * 1024 * 1024


def deposit_kernel(tiles_ref, live_ref, off_ref, vel_ref, aff_ref, mass_ref, cell_ref,
                   acc_ref, down_ref, up_ref, *, blocks, unroll):
    step = pl.program_id(0)

    @pl.when(step == 0)
    def _():
        acc_ref[...] = jnp.zeros_like(acc_ref)

    slots = lax.broadcasted_iota(jnp.int32, (LANES, LANES), 0)
    half = lax.broadcasted_iota(jnp.int32, (8, LANES), 0) // 4
    live = live_ref[0]

    def group(i, carry):
        sums = []
        for u in range(unroll):
            b = i * unroll + u
            m = vel_ref[b]
            for j in range(3):
                m = m - aff_ref[b, pl.ds(j, 3, stride=3), :] * off_ref[b, j:j + 1, :]
            active = (step * blocks + b < live).astype(jnp.float32)
            w = mass_ref[pl.ds(b, 1), :] * active
            x = jnp.concatenate([w * m, w], axis=0)
            c = cell_ref[pl.ds(b, 1), :]
            x = jnp.where((c >> 7) == half, jnp.concatenate([x, x], axis=0), 0.0)
            high = x.astype(jnp.bfloat16).astype(jnp.float32)
            parts = jnp.concatenate([high, x - high], axis=0).astype(jnp.bfloat16)
            select = jnp.where((c & (LANES - 1)) == slots, 1.0, 0.0).astype(jnp.bfloat16)
            r = lax.dot_general(parts, select, (((1,), (1,)), ((), ())),
                                preferred_element_type=jnp.float32)
            sums.append(r[:8] + r[8:])
        for u in range(unroll):
            t = tiles_ref[step * blocks + i * unroll + u]
            acc_ref[t] += sums[u]
        return carry

    lax.fori_loop(0, blocks // unroll, group, 0)

    @pl.when(step == pl.num_programs(0) - 1)
    def _():
        n = down_ref.shape[0]
        down_ref[...] = acc_ref[acc_ref.shape[0] - n:]
        up_ref[...] = acc_ref[:n]


def picked_velocity(tile, c):
    where = jnp.broadcast_to(c & (LANES - 1), tile.shape)
    g = jnp.take_along_axis(tile, where, axis=1)
    return jnp.where(c >= LANES, g[4:7], g[0:3])


def write_state(out_ref, b, v, off_ref, src):
    o = off_ref[src]
    out_ref[b, 0:3, :] = o + time_step * v
    out_ref[b, 3:6, :] = v
    for j in range(3):
        out_ref[b, pl.ds(6 + j, 3, stride=3), :] = (-4.0 * v) * off_ref[src, j:j + 1, :]


def grid_kernel(tiles_ref, lists_ref, counts_ref, ends_ref, acc_ref, before_ref, after_ref,
                off_ref, mass_ref, cell_ref, settled_ref, cols_ref, rec_ref, speed_ref,
                *, row, margin):
    total = acc_ref.shape[0]
    side = before_ref.shape[0]
    rid = lax.broadcasted_iota(jnp.int32, (1, 8, LANES), 1)
    pull = jnp.zeros((1, 8, LANES), jnp.float32)
    for k in range(3):
        pull = jnp.where(rid % 4 == k, time_step * gravity_pull[k], pull)

    def speed_of(x):
        mass = jnp.where(rid < 4, x[:, 3:4, :], x[:, 7:8, :])
        return x / jnp.maximum(mass, 1.0) + pull

    first = ends_ref[0]
    last = ends_ref[1]
    inner = side - row
    chunk = 8

    def middle(i, carry):
        at = inner + i * chunk
        speed_ref[pl.ds(row + at, chunk)] = speed_of(acc_ref[pl.ds(at, chunk)])
        return carry

    lax.fori_loop(0, (total - 2 * inner) // chunk, middle, 0)

    keep_first = 1.0 - first.astype(jnp.float32)
    keep_last = 1.0 - last.astype(jnp.float32)

    def outer(i, carry):
        at = i * chunk
        speed_ref[pl.ds(at, chunk)] = speed_of(before_ref[pl.ds(at, chunk)]) * keep_first
        end = total + row + at
        speed_ref[pl.ds(end, chunk)] = (
            speed_of(after_ref[pl.ds(inner + at, chunk)]) * keep_last)
        return carry

    lax.fori_loop(0, row // chunk, outer, 0)

    def seam(i, carry):
        at = i * chunk
        beyond = at < margin * row
        x = speed_of(acc_ref[pl.ds(at, chunk)] + before_ref[pl.ds(row + at, chunk)])
        speed_ref[pl.ds(row + at, chunk)] = x * jnp.where(beyond, keep_first, 1.0)
        far = total - inner + at
        past = at >= inner - margin * row
        y = speed_of(acc_ref[pl.ds(far, chunk)] + after_ref[pl.ds(at, chunk)])
        speed_ref[pl.ds(row + far, chunk)] = y * jnp.where(past, keep_last, 1.0)
        return carry

    lax.fori_loop(0, inner // chunk, seam, 0)

    def smooth(i, carry):
        at = i * chunk
        s = speed_ref[pl.ds(row + at, chunk)]
        settled_ref[pl.ds(at, chunk)] = s + viscosity * (
            speed_ref[pl.ds(2 * row + at, chunk)] + speed_ref[pl.ds(at, chunk)] - 2.0 * s)
        return carry

    lax.fori_loop(0, total // chunk, smooth, 0)

    planes = cols_ref.shape[1]
    flat = settled_ref.reshape(total * 8, LANES)

    def column(tc, carry):
        for group in range(planes // 8):
            for h in range(2):
                for k in range(3):
                    start = (margin + group * 8) * row * 8 + tc * 8 + h * 4 + k
                    x = flat[pl.ds(start, 8, stride=row * 8), :]
                    at = pl.multiple_of(tc * TILE + h * LANES, LANES)
                    cols_ref[k, group * 8:group * 8 + 8, pl.ds(at, LANES)] = x
        return carry

    lax.fori_loop(0, row, column, 0)

    slots = lists_ref.shape[1]

    def record(i, carry):
        for way in range(2):
            b = lists_ref[way, i]
            keep = jnp.where(i < counts_ref[way], 1.0, 0.0)
            v = picked_velocity(settled_ref[tiles_ref[b]], cell_ref[pl.ds(b, 1), :])
            o = off_ref[b]
            at = way * slots + i
            rec_ref[at, 0:3, :] = (o + time_step * v) * keep
            rec_ref[at, 3:6, :] = v * keep
            for j in range(3):
                rec_ref[at, pl.ds(6 + j, 3, stride=3), :] = (
                    (-4.0 * v) * off_ref[b, j:j + 1, :] * keep)
            rec_ref[at, 15:16, :] = mass_ref[pl.ds(b, 1), :] * keep
        return carry

    lax.fori_loop(0, slots, record, 0)


def update_kernel(tiles_ref, off_ref, cell_ref, settled_ref, out_ref, *, blocks, unroll):
    step = pl.program_id(0)

    def group(i, carry):
        for u in range(unroll):
            b = i * unroll + u
            t = tiles_ref[step * blocks + b]
            v = picked_velocity(settled_ref[t], cell_ref[pl.ds(b, 1), :])
            write_state(out_ref, b, v, off_ref, b)
        return carry

    lax.fori_loop(0, blocks // unroll, group, 0)


def body(offsets, velocity, affine, particle_mass, cell_in_tile, block_tile, live_blocks,
         send_lists, send_counts):
    axes = ("slab", "deal")
    slabs, deals = lax.axis_size("slab"), lax.axis_size("deal")
    count = slabs * deals
    slab, deal = lax.axis_index("slab"), lax.axis_index("deal")
    nb = offsets.shape[0]
    row = PLANE // TILE
    planes = PX // deals
    share = planes * row
    margin = -(-max(share // 16, 1) // row)
    total = (planes + 2 * margin) * row
    side = (2 * margin + 1) * row
    f32 = jnp.float32

    tiles = block_tile - (deal * share - margin * row)
    blocks = 128 if nb % 128 == 0 else nb
    unroll = 8
    params = pltpu.CompilerParams(vmem_limit_bytes=VMEM_LIMIT)
    smem = pl.BlockSpec(memory_space=pltpu.SMEM)
    vmem = pl.BlockSpec(memory_space=pltpu.VMEM)

    def per_block(*tail):
        return pl.BlockSpec((blocks,) + tail, lambda i: (i,) + (0,) * len(tail))

    def whole(*shape):
        return pl.BlockSpec(shape, lambda i: (0,) * len(shape))

    acc, down, up = pl.pallas_call(
        functools.partial(deposit_kernel, blocks=blocks, unroll=unroll),
        grid=(nb // blocks,),
        in_specs=[smem, smem, per_block(3, LANES), per_block(3, LANES), per_block(9, LANES),
                  per_block(LANES), per_block(LANES)],
        out_specs=[whole(total, 8, LANES), whole(side, 8, LANES), whole(side, 8, LANES)],
        out_shape=[jax.ShapeDtypeStruct((n, 8, LANES), f32) for n in (total, side, side)],
        compiler_params=params,
        name="deposit",
    )(tiles, live_blocks.reshape(1), offsets, velocity, affine, particle_mass, cell_in_tile)

    before = lax.ppermute(down, axes, [(i, i + 1) for i in range(count - 1)])
    after = lax.ppermute(up, axes, [(i + 1, i) for i in range(count - 1)])

    place = slab * deals + deal
    ends = jnp.stack([place == 0, place == count - 1]).astype(jnp.int32)
    mig = send_lists.shape[-1]
    settled, cols, records = pl.pallas_call(
        functools.partial(grid_kernel, row=row, margin=margin),
        in_specs=[smem] * 4 + [vmem] * 6,
        out_specs=[vmem] * 3,
        out_shape=[jax.ShapeDtypeStruct((total, 8, LANES), f32),
                   jax.ShapeDtypeStruct((3, planes, PLANE), f32),
                   jax.ShapeDtypeStruct((2 * mig, 16, LANES), f32)],
        scratch_shapes=[pltpu.VMEM((total + 2 * row, 8, LANES), f32)],
        compiler_params=params,
        name="grid_step",
    )(tiles, send_lists[0, 0], send_counts.reshape(2), ends, acc, before, after,
      offsets, particle_mass, cell_in_tile)

    from_left = lax.ppermute(records[:mig], "slab", [(i, i + 1) for i in range(slabs - 1)])
    from_right = lax.ppermute(records[mig:], "slab", [(i + 1, i) for i in range(slabs - 1)])

    width = PLANE // deals
    pieces = [lax.dynamic_slice_in_dim(cols, deal * width, width, axis=2)]
    for k in range(1, deals):
        chosen = lax.dynamic_slice_in_dim(cols, ((deal + k) % deals) * width, width, axis=2)
        pieces.append(lax.ppermute(chosen, "deal", [(i, (i + k) % deals) for i in range(deals)]))

    state = pl.pallas_call(
        functools.partial(update_kernel, blocks=blocks, unroll=unroll),
        grid=(nb // blocks,),
        in_specs=[smem, per_block(3, LANES), per_block(LANES), whole(total, 8, LANES)],
        out_specs=per_block(15, LANES),
        out_shape=jax.ShapeDtypeStruct((nb, 15, LANES), f32),
        compiler_params=params,
        cost_estimate=pl.CostEstimate(flops=nb * 15 * LANES * 4,
                                      bytes_accessed=nb * 20 * LANES * 4, transcendentals=0),
        name="update",
    )(tiles, offsets, cell_in_tile, settled)

    arrivals = jnp.stack([from_left, from_right], axis=0)[None, None]
    grid = jnp.zeros((3, PX, width), f32)
    for k in range(deals):
        grid = lax.dynamic_update_slice_in_dim(
            grid, pieces[k], ((deal - k) % deals) * planes, axis=1)
    return state, arrivals, grid


def solution(mesh):
    placed = (
        P(("slab", "deal"), None, None),
        P(("slab", "deal"), None, None),
        P(("slab", "deal"), None, None),
        P(("slab", "deal"), None),
        P(("slab", "deal"), None),
        P(("slab", "deal")),
        P("slab", "deal"),
        P("slab", "deal", None, None),
        P("slab", "deal", None),
    )
    return jax.shard_map(
        body,
        mesh=mesh,
        in_specs=placed,
        out_specs=(
            P(("slab", "deal"), None, None),
            P("slab", "deal", None, None, None, None),
            P(None, "slab", "deal"),
        ),
        check_vma=False,
    )
```

time: 522 us -> 121 us (0.23)
  matrix products: 188 us -> 0 us
  waiting for transfers between devices: 161 us -> 14.8 us
  local copies, waits for them, and re-layouts: 112 us -> 30.1 us
  Pallas kernels: 0 us -> 54.8 us
  other arithmetic: 30.7 us -> 1.77 us
  between operations: 15 us -> 1.5 us
  starting transfers between devices: 11.5 us -> 17.5 us
    dot_general x24 -> x0, matrix products: 188 us -> none  [the longest x8 71.3 us: gather_group(): return jnp.einsum('cbk,bpk->bcp', chosen, selector, precision=highest)]
    reduce_scatter x1 -> x0, waiting for transfers between devices: 88.5 us -> none  [body(): lax.psum_scatter(partial_grid, 'deal', scatter_dimension=2, tiled=True)]
    all_gather x1 -> x0, waiting for transfers between devices: 70.6 us -> none  [body(): settled = lax.all_gather(own_share, 'deal', axis=2, tiled=True)]
    pallas_call x0 -> x3, Pallas kernels: none -> 54.8 us  [the longest x1 35.9 us: body(): pl.pallas_call(functools.partial(deposit_kernel, blocks=blocks, unroll=un...]
    gather x9 -> x0, local copies, waits for them, and re-layouts: 44.2 us -> none  [the longest x8 40.3 us: gather_group(): chosen = jnp.take(tiles_view, part_tiles, axis=1)]
    eq x24 -> x0, local copies, waits for them, and re-layouts: 19.1 us -> none  [the longest x8 6.75 us: scatter_group(): selector = (part_cells[:, :, None] == tile_slots).astype(jnp.float32)]
    reshape x2 -> x0, local copies, waits for them, and re-layouts: 16.5 us -> none  [the longest x1 9.46 us: body(): partial_grid = accumulated.reshape(4, PX, PLANE)]
    ppermute x4 -> x7, waiting for transfers between devices: 1.7 us -> 14.8 us  [the longest x1 8.66 us: body(): before = lax.ppermute(down, axes, [(i, i + 1) for i in range(count - 1)])]
  transfers between devices with their start and end apart: 6 -> 7, of which waited for: 4 -> 2; matrix products, arithmetic and copies ran while one was open for 1% -> 8% of each run, Pallas kernels for 0% -> 11%
where the time goes in v1:
time: 121 us
  Pallas kernels  54.8 us (45%)
  local copies, waits for them, and re-layouts  30.1 us (25%)
  starting transfers between devices  17.5 us (14%)
  waiting for transfers between devices  14.8 us (12%)
  other arithmetic  1.77 us (1%)
  between operations  1.5 us (1%)
    pallas_call x1, Pallas kernels, body(): pl.pallas_call(functools.partial(deposit_kernel, blocks=blocks, unroll=un...  35.9 us
    unnamed x32, local copies, waits for them, and re-layouts  26 us
    pallas_call x1, Pallas kernels, body(): pl.pallas_call(functools.partial(update_kernel, blocks=blocks, unroll=unr...  13.3 us
    ppermute x1, waiting for transfers between devices, body(): before = lax.ppermute(down, axes, [(i, i + 1) for i in range(count - 1)])  8.66 us
    ppermute x1, waiting for transfers between devices, body(): after = lax.ppermute(up, axes, [(i + 1, i) for i in range(count - 1)])  6.18 us
    pallas_call x1, Pallas kernels, body(): pl.pallas_call(functools.partial(grid_kernel, row=row, margin=margin), in...  5.63 us
    ppermute x1, starting transfers between devices, body(): lax.ppermute(records[:mig], 'slab', [(i, i + 1) for i in range(slabs - 1)])  4.92 us
    ppermute x1, starting transfers between devices, body(): before = lax.ppermute(down, axes, [(i, i + 1) for i in range(count - 1)])  3.88 us
  transfers between devices with their start and end apart: 7, of which 2 were waited for; matrix products, arithmetic and copies ran while one was open for 8% of the time, Pallas kernels for 11%

profile of v1, /device:TPU:1, one launch (start us, length us, event | category | flops | bytes accessed | tf_op | source)
XLA Modules:
  0.0 120.5 jit_solution(17162921463535077378)
XLA Ops:
  1.3 2.6 %copy.16.off_ref = f32[1024,3,128]{2,1,0:T(4,128)S(1)} copy(f32[1024,3,128]{2,0,1:T(8,128)} %param.9) | data formatting | bytes 3145728 | tf_op args[0]
  3.9 3.8 %copy.13.vel_ref = f32[1024,3,128]{2,1,0:T(4,128)} copy(f32[1024,3,128]{2,0,1:T(8,128)} %param.10) | data formatting | bytes 3145728 | tf_op args[1]
  7.8 6.2 %copy.14.aff_ref = f32[1024,9,128]{2,1,0:T(8,128)} copy(f32[1024,9,128]{2,0,1:T(8,128)S(1)} %copy-done.9) | data formatting | bytes 9437184 | tf_op args[2]
  14.0 1.6 %copy-done = f32[1024,3,128]{2,1,0:T(4,128)S(1)} copy-done((f32[1024,3,128]{2,1,0:T(4,128)S(1)}, f32[1024,3,128]{2,1,0:T(4,128)}, u32[]{:S(2)}) %copy-start) | copy-done | bytes 1572888
  15.6 35.9 %deposit.1 = (f32[576,8,128]{2,1,0:T(8,128)S(1)}, f32[96,8,128]{2,1,0:T(8,128)}, f32[96,8,128]{2,1,0:T(8,128)}) custom-call(s32[1024]{0:T(1024)S(1)} %broadcast_subtract_fusion.tiles_ref, s32[1]{0:T(128)} %bitcast.9.live_ref, f32[1024,3,128]{2,1,0:T(4,128)S(1)} %copy.16.off_ref, f32[1024,3,128]{2,1,0:T(4,128)S(1)} %copy-done, f32[1024,9,128]{2,1,0:T(8,128)} %copy.14.aff_ref, ...), custom_call_target="tpu_custom_call" | custom-call | tf_op jit(solution)/shard_map/deposit/pallas_call | solution.py:218
  51.5 1.4 %copy-done.2 = f32[576,8,128]{2,1,0:T(8,128)} copy-done((f32[576,8,128]{2,1,0:T(8,128)}, f32[576,8,128]{2,1,0:T(8,128)S(1)}, u32[]{:S(2)}) %copy-start.2) | copy-done | bytes 2359320
  52.9 3.9 %collective-permute-start = (f32[96,8,128]{2,1,0:T(8,128)}, f32[96,8,128]{2,1,0:T(8,128)S(1)}, u32[]{:S(2)}, u32[]{:S(2)}) collective-permute-start(f32[96,8,128]{2,1,0:T(8,128)} %get-tuple-element.10), channel_id=1, source_target_pairs={{0,1},{1,2},{2,3},{3,4},{4,5},{5,6},{6,7},{7,8},{8,9},{9,10},{10,1... | collective-permute-start | bytes 1179656 | tf_op jit(solution)/shard_map/ppermute | solution.py:229
  56.8 3.5 %collective-permute-start.1 = (f32[96,8,128]{2,1,0:T(8,128)}, f32[96,8,128]{2,1,0:T(8,128)}, u32[]{:S(2)}, u32[]{:S(2)}) collective-permute-start(f32[96,8,128]{2,1,0:T(8,128)} %get-tuple-element.11), channel_id=1, source_target_pairs={{1,0},{2,1},{3,2},{4,3},{5,4},{6,5},{7,6},{8,7},{9,8},{10,9},{11,1... | collective-permute-start | bytes 1179656 | tf_op jit(solution)/shard_map/ppermute | solution.py:230
  60.4 8.7 %collective-permute-done.before_ref = f32[96,8,128]{2,1,0:T(8,128)S(1)} collective-permute-done((f32[96,8,128]{2,1,0:T(8,128)}, f32[96,8,128]{2,1,0:T(8,128)S(1)}, u32[]{:S(2)}, u32[]{:S(2)}) %collective-permute-start) | collective-permute-done | bytes 393248 | tf_op jit(solution)/shard_map/ppermute | solution.py:229
  69.1 6.2 %collective-permute-done.1.after_ref = f32[96,8,128]{2,1,0:T(8,128)} collective-permute-done((f32[96,8,128]{2,1,0:T(8,128)}, f32[96,8,128]{2,1,0:T(8,128)}, u32[]{:S(2)}, u32[]{:S(2)}) %collective-permute-start.1) | collective-permute-done | bytes 393248 | tf_op jit(solution)/shard_map/ppermute | solution.py:230
  75.3 1.7 %copy-done.3 = f32[576,8,128]{2,1,0:T(8,128)S(1)} copy-done((f32[576,8,128]{2,1,0:T(8,128)S(1)}, f32[576,8,128]{2,1,0:T(8,128)}, u32[]{:S(2)}) %copy-start.3) | copy-done | bytes 2359320
  76.9 5.6 %grid_step.1 = (f32[576,8,128]{2,1,0:T(8,128)S(1)}, f32[3,16,8192]{2,1,0:T(8,128)S(1)}, f32[32,16,128]{2,1,0:T(8,128)S(1)}) custom-call(s32[1024]{0:T(1024)S(1)} %broadcast_subtract_fusion.tiles_ref, s32[2,16]{1,0:T(2,128)S(1)} %bitcast.10, s32[2]{0:T(128)S(1)} %bitcast.11, s32[2]{0:T(128)S(1)} %add_convert_fusion.ends_ref, f32[576,8,128]{2,1,0:T(8,128)S(1)} %copy-done.3, ...), custom_call_target="tpu_custom_call" | custom-call | tf_op jit(solution)/shard_map/grid_step/pallas_call | solution.py:235
  82.8 1.2 constant_dynamic-slice_fusion
  84.1 1.2 collective-permute-start.4
  85.9 4.9 %collective-permute-start.2 = (f32[16,16,128]{2,1,0:T(8,128)}, f32[16,16,128]{2,1,0:T(8,128)}, u32[]{:S(2)}, u32[]{:S(2)}) collective-permute-start(f32[16,16,128]{2,1,0:T(8,128)} %get-tuple-element.22), channel_id=1, source_target_pairs={{0,4},{4,8},{8,12},{12,16},{16,20},{20,24},{24,28},{1,5},{5,9},{9,... | collective-permute-start | bytes 393224 | tf_op jit(solution)/shard_map/ppermute | solution.py:248
  90.9 1.9 %collective-permute-start.3 = (f32[16,16,128]{2,1,0:T(8,128)S(1)}, f32[16,16,128]{2,1,0:T(8,128)}, u32[]{:S(2)}, u32[]{:S(2)}) collective-permute-start(f32[16,16,128]{2,1,0:T(8,128)S(1)} %get-tuple-element.23), channel_id=1, source_target_pairs={{4,0},{8,4},{12,8},{16,12},{20,16},{24,20},{28,24},{5,1},{9,5},{13... | collective-permute-start | bytes 393224 | tf_op jit(solution)/shard_map/ppermute | solution.py:249
  93.2 1.8 %collective-permute-start.6 = (f32[3,16,2048]{2,1,0:T(8,128)S(1)}, f32[3,16,2048]{2,1,0:T(8,128)S(1)}, u32[]{:S(2)}, u32[]{:S(2)}) collective-permute-start(f32[3,16,2048]{2,1,0:T(8,128)S(1)} %get-tuple-element.18), channel_id=1, source_target_pairs={{0,3},{1,0},{2,1},{3,2},{4,7},{5,4},{6,5},{7,6},{8,11},{9,8},{10,9... | collective-permute-start | bytes 1179656 | tf_op jit(solution)/shard_map/ppermute | solution.py:255
  95.0 1.7 %copy-done.5 = f32[576,8,128]{2,1,0:T(8,128)S(1)} copy-done((f32[576,8,128]{2,1,0:T(8,128)S(1)}, f32[576,8,128]{2,1,0:T(8,128)}, u32[]{:S(2)}) %copy-start.5) | copy-done | bytes 2359320
  96.6 13.3 %update.1 = f32[1024,15,128]{2,1,0:T(8,128)S(1)} custom-call(s32[1024]{0:T(1024)S(1)} %broadcast_subtract_fusion.tiles_ref, f32[1024,3,128]{2,1,0:T(4,128)S(1)} %copy.16.off_ref, s32[1024,128]{1,0:T(8,128)S(1)} %copy-done.1, f32[576,8,128]{2,1,0:T(8,128)S(1)} %copy-done.5), custom_call_target="tpu_custom_call" | custom-call | flops 7864320 | bytes 10485760 | tf_op jit(solution)/shard_map/update/pallas_call | solution.py:257
  109.9 5.6 %copy.17 = f32[1024,15,128]{2,0,1:T(8,128)} copy(f32[1024,15,128]{2,1,0:T(8,128)S(1)} %update.1) | data formatting | bytes 15728640
  115.5 1.7 %maximum_bitcast_fusion = f32[1,1,2,16,16,128]{5,4,3,2,1,0:T(8,128)} fusion(f32[1,16,16,128]{3,2,1,0:T(8,128)} %bitcast.6, f32[1,16,16,128]{3,2,1,0:T(8,128)} %bitcast.5), kind=kLoop, calls=%fused_computation.1 | loop fusion | flops 65536 | bytes 524288 | tf_op jit(solution)/shard_map/broadcast_in_dim | solution.py:269
  117.2 1.0 constant_dynamic-update-slice_fusion.1
  118.3 1.0 constant_dynamic-update-slice_fusion
  119.4 1.1 copy-done.12
  (34 shorter events, 1.6 us)
Async XLA Ops:
  1.3 6.5 %copy-start.9 = (f32[1024,9,128]{2,0,1:T(8,128)S(1)}, f32[1024,9,128]{2,0,1:T(8,128)}, u32[]{:S(2)}) copy-start(f32[1024,9,128]{2,0,1:T(8,128)} %param.11) | copy-start | bytes 14155780
  7.7 6.2 %copy-start.13 = (s32[1024]{0:T(1024)S(1)}, s32[1024]{0:T(1024)}, u32[]{:S(2)}) copy-start(s32[1024]{0:T(1024)} %param.14) | copy-start | bytes 12292
  7.7 6.2 %copy-start.1 = (s32[1024,128]{1,0:T(8,128)S(1)}, s32[1024,128]{1,0:T(8,128)}, u32[]{:S(2)}) copy-start(s32[1024,128]{1,0:T(8,128)} %cell_ref.5) | copy-start | bytes 1572868
  7.7 6.2 %copy-start.6 = (f32[1024,128]{1,0:T(8,128)S(1)}, f32[1024,128]{1,0:T(8,128)}, u32[]{:S(2)}) copy-start(f32[1024,128]{1,0:T(8,128)} %mass_ref.3) | copy-start | bytes 1572868
  14.0 1.6 %copy-start = (f32[1024,3,128]{2,1,0:T(4,128)S(1)}, f32[1024,3,128]{2,1,0:T(4,128)}, u32[]{:S(2)}) copy-start(f32[1024,3,128]{2,1,0:T(4,128)} %copy.13.vel_ref) | copy-start | bytes 4718596
  15.6 59.7 %copy-start.7 = (s32[1,1,2,16]{3,2,1,0:T(2,128)S(1)}, s32[1,1,2,16]{3,2,1,0:T(2,128)}, u32[]{:S(2)}) copy-start(s32[1,1,2,16]{3,2,1,0:T(2,128)} %param.16) | copy-start | bytes 388
  15.6 59.7 %copy-start.8 = (s32[1,1,2]{2,1,0:T(1,128)S(1)}, s32[1,1,2]{2,1,0:T(1,128)}, u32[]{:S(2)}) copy-start(s32[1,1,2]{2,1,0:T(1,128)} %param.17) | copy-start | bytes 28
  51.5 1.4 %copy-start.2 = (f32[576,8,128]{2,1,0:T(8,128)}, f32[576,8,128]{2,1,0:T(8,128)S(1)}, u32[]{:S(2)}) copy-start(f32[576,8,128]{2,1,0:T(8,128)S(1)} %get-tuple-element.9.acc_ref) | copy-start | bytes 7077892
  52.9 16.2 %collective-permute-start = (f32[96,8,128]{2,1,0:T(8,128)}, f32[96,8,128]{2,1,0:T(8,128)S(1)}, u32[]{:S(2)}, u32[]{:S(2)}) collective-permute-start(f32[96,8,128]{2,1,0:T(8,128)} %get-tuple-element.10), channel_id=1, source_target_pairs={{0,1},{1,2},{2,3},{3,4},{4,5},{5,6},{6,7},{7,8},{8,9},{9,10},{10,1... | collective-permute-start | bytes 1179656 | tf_op jit(solution)/shard_map/ppermute | solution.py:229
  56.8 18.5 %collective-permute-start.1 = (f32[96,8,128]{2,1,0:T(8,128)}, f32[96,8,128]{2,1,0:T(8,128)}, u32[]{:S(2)}, u32[]{:S(2)}) collective-permute-start(f32[96,8,128]{2,1,0:T(8,128)} %get-tuple-element.11), channel_id=1, source_target_pairs={{1,0},{2,1},{3,2},{4,3},{5,4},{6,5},{7,6},{8,7},{9,8},{10,9},{11,1... | collective-permute-start | bytes 1179656 | tf_op jit(solution)/shard_map/ppermute | solution.py:230
  75.3 1.7 %copy-start.3 = (f32[576,8,128]{2,1,0:T(8,128)S(1)}, f32[576,8,128]{2,1,0:T(8,128)}, u32[]{:S(2)}) copy-start(f32[576,8,128]{2,1,0:T(8,128)} %copy-done.2) | copy-start | bytes 7077892
  82.6 1.5 %copy-start.4 = (f32[576,8,128]{2,1,0:T(8,128)}, f32[576,8,128]{2,1,0:T(8,128)S(1)}, u32[]{:S(2)}) copy-start(f32[576,8,128]{2,1,0:T(8,128)S(1)} %get-tuple-element.12.settled_ref) | copy-start | bytes 7077892
  84.1 1.8 %copy-start.10 = (f32[3,64,2048]{2,1,0:T(8,128)}, f32[3,64,2048]{2,1,0:T(8,128)S(1)}, u32[]{:S(2)}) copy-start(f32[3,64,2048]{2,1,0:T(8,128)S(1)} %get-tuple-element.21) | copy-start | bytes 4718596
  84.1 33.1 %collective-permute-start.4 = (f32[3,16,2048]{2,1,0:T(8,128)}, f32[3,16,2048]{2,1,0:T(8,128)}, u32[]{:S(2)}, u32[]{:S(2)}) collective-permute-start(f32[3,16,2048]{2,1,0:T(8,128)} %get-tuple-element.20), channel_id=1, source_target_pairs={{0,1},{1,2},{2,3},{3,0},{4,5},{5,6},{6,7},{7,4},{8,9},{9,10},{10,1... | collective-permute-start | bytes 1179656 | tf_op jit(solution)/shard_map/ppermute | solution.py:255
  85.9 29.6 %collective-permute-start.2 = (f32[16,16,128]{2,1,0:T(8,128)}, f32[16,16,128]{2,1,0:T(8,128)}, u32[]{:S(2)}, u32[]{:S(2)}) collective-permute-start(f32[16,16,128]{2,1,0:T(8,128)} %get-tuple-element.22), channel_id=1, source_target_pairs={{0,4},{4,8},{8,12},{12,16},{16,20},{20,24},{24,28},{1,5},{5,9},{9,... | collective-permute-start | bytes 393224 | tf_op jit(solution)/shard_map/ppermute | solution.py:248
  90.9 24.7 %collective-permute-start.3 = (f32[16,16,128]{2,1,0:T(8,128)S(1)}, f32[16,16,128]{2,1,0:T(8,128)}, u32[]{:S(2)}, u32[]{:S(2)}) collective-permute-start(f32[16,16,128]{2,1,0:T(8,128)S(1)} %get-tuple-element.23), channel_id=1, source_target_pairs={{4,0},{8,4},{12,8},{16,12},{20,16},{24,20},{28,24},{5,1},{9,5},{13... | collective-permute-start | bytes 393224 | tf_op jit(solution)/shard_map/ppermute | solution.py:249
  92.8 25.5 %collective-permute-start.5 = (f32[3,16,2048]{2,1,0:T(8,128)S(1)}, f32[3,16,2048]{2,1,0:T(8,128)}, u32[]{:S(2)}, u32[]{:S(2)}) collective-permute-start(f32[3,16,2048]{2,1,0:T(8,128)S(1)} %get-tuple-element.19), channel_id=1, source_target_pairs={{0,2},{1,3},{2,0},{3,1},{4,6},{5,7},{6,4},{7,5},{8,10},{9,11},{10,... | collective-permute-start | bytes 1179656 | tf_op jit(solution)/shard_map/ppermute | solution.py:255
  93.2 26.1 %collective-permute-start.6 = (f32[3,16,2048]{2,1,0:T(8,128)S(1)}, f32[3,16,2048]{2,1,0:T(8,128)S(1)}, u32[]{:S(2)}, u32[]{:S(2)}) collective-permute-start(f32[3,16,2048]{2,1,0:T(8,128)S(1)} %get-tuple-element.18), channel_id=1, source_target_pairs={{0,3},{1,0},{2,1},{3,2},{4,7},{5,4},{6,5},{7,6},{8,11},{9,8},{10,9... | collective-permute-start | bytes 1179656 | tf_op jit(solution)/shard_map/ppermute | solution.py:255
  95.0 1.7 %copy-start.5 = (f32[576,8,128]{2,1,0:T(8,128)S(1)}, f32[576,8,128]{2,1,0:T(8,128)}, u32[]{:S(2)}) copy-start(f32[576,8,128]{2,1,0:T(8,128)} %copy-done.4) | copy-start | bytes 7077892
  109.9 7.3 %copy-start.11 = (f32[3,64,2048]{2,1,0:T(8,128)S(1)}, f32[3,64,2048]{2,1,0:T(8,128)}, u32[]{:S(2)}) copy-start(f32[3,64,2048]{2,1,0:T(8,128)} %copy-done.10) | copy-start | bytes 4718596
  119.4 1.1 copy-start.12

commit v2 on v1

v2 whole, which is shorter than its diff:
```python
import functools

import jax
import jax.numpy as jnp
from jax import lax
from jax.experimental import pallas as pl
from jax.experimental.pallas import tpu as pltpu
from jax.sharding import PartitionSpec as P

PX = 64
PLANE = 8192
TILE = 256
LANES = 128
SPAN = 32

time_step = 0.1
viscosity = 0.2
gravity_pull = (3.0, 0.0, -5.0)

VMEM_LIMIT = 40 * 1024 * 1024


def deposit_span(at, first, start, stop, ins, out_ref, shift, tiles_ref, parts_ref):
    off_ref, vel_ref, aff_ref, mass_ref, cell_ref = ins
    slots = lax.broadcasted_iota(jnp.int32, (LANES, LANES), 0).astype(jnp.float32)
    slots = slots.astype(jnp.bfloat16)
    one, zero = jnp.ones((), jnp.bfloat16), jnp.zeros((), jnp.bfloat16)
    spot = lax.broadcasted_iota(jnp.int32, (8, LANES), 0)
    sums = []
    for g in range(SPAN // 8):
        rows = pl.ds(pl.multiple_of(at + g * 8, 8), 8)
        offset = [off_ref[k, rows, :] for k in range(3)]
        block = first + at + g * 8 + spot
        w = jnp.where((block >= start) & (block < stop), mass_ref[rows, :], 0.0)
        values = []
        for k in range(3):
            m = vel_ref[k, rows, :]
            for j in range(3):
                m = m - aff_ref[3 * k + j, rows, :] * offset[j]
            values.append(w * m)
        values.append(w)
        c = cell_ref[rows, :]
        upper = c >= LANES
        base = g * LANES
        for k in range(4):
            high = values[k].astype(jnp.bfloat16).astype(jnp.float32)
            low = values[k] - high
            for s, part in enumerate((high, low)):
                put = base + s * 64 + k * 8
                parts_ref[put:put + 8, :] = jnp.where(upper, 0.0, part)
                parts_ref[put + 32:put + 40, :] = jnp.where(upper, part, 0.0)
        lane = (c & (LANES - 1)).astype(jnp.float32)
        for u in range(8):
            lhs = parts_ref[pl.ds(base + u, 16, stride=8), :].astype(jnp.bfloat16)
            row = jnp.broadcast_to(lane[u:u + 1], (16, LANES)).astype(jnp.bfloat16)
            select = jnp.where(jnp.concatenate([row] * 8, axis=0) == slots, one, zero)
            r = lax.dot_general(lhs, select, (((1,), (1,)), ((), ())),
                                preferred_element_type=jnp.float32)
            sums.append(r[:8] + r[8:])
    for u in range(SPAN):
        block = first + at + u
        t = tiles_ref[block] - shift
        inside = (block >= start) & (block < stop)
        out_ref[jnp.where(inside, t, 0)] += sums[u]


def deposit_range(blocks, start, stop, ins, out_ref, shift, tiles_ref, parts_ref):
    first = pl.program_id(0) * blocks
    low = lax.div(jnp.clip(start - first, 0, blocks), SPAN)
    high = lax.div(jnp.clip(stop - first, 0, blocks) + SPAN - 1, SPAN)
    high = jnp.where(stop > start, high, low)

    def step(i, carry):
        deposit_span(i * SPAN, first, start, stop, ins, out_ref, shift, tiles_ref, parts_ref)
        return carry

    lax.fori_loop(low, high, step, 0)


def edge_kernel(marks_ref, tiles_ref, *refs, blocks, shift):
    *ins, up_ref, down_ref, parts_ref = refs

    @pl.when(pl.program_id(0) == 0)
    def _():
        up_ref[...] = jnp.zeros_like(up_ref)
        down_ref[...] = jnp.zeros_like(down_ref)

    deposit_range(blocks, 0, marks_ref[0], ins, up_ref, 0, tiles_ref, parts_ref)
    deposit_range(blocks, marks_ref[1], marks_ref[2], ins, down_ref, shift, tiles_ref, parts_ref)


def middle_kernel(marks_ref, tiles_ref, *refs, blocks, shift):
    *ins, mid_ref, parts_ref = refs

    @pl.when(pl.program_id(0) == 0)
    def _():
        mid_ref[...] = jnp.zeros_like(mid_ref)

    deposit_range(blocks, marks_ref[0], marks_ref[1], ins, mid_ref, shift, tiles_ref, parts_ref)


def update_kernel(tiles_ref, off_ref, cell_ref, settled_ref, out_ref, picked_ref, *, blocks):
    first = pl.program_id(0) * blocks

    def step(i, carry):
        for g in range(SPAN // 8):
            rows = pl.ds(pl.multiple_of(i * SPAN + g * 8, 8), 8)
            c = cell_ref[rows, :]
            lane = c & (LANES - 1)
            base = g * 64
            for u in range(8):
                tile = settled_ref[tiles_ref[first + i * SPAN + g * 8 + u]]
                where = jnp.broadcast_to(lane[u:u + 1], (8, LANES))
                put = base + u * 8
                picked_ref[put:put + 8, :] = jnp.take_along_axis(tile, where, axis=1)
            offset = [off_ref[k, rows, :] for k in range(3)]
            for k in range(3):
                v = jnp.where(c >= LANES, picked_ref[pl.ds(base + 4 + k, 8, stride=8), :],
                              picked_ref[pl.ds(base + k, 8, stride=8), :])
                out_ref[k, rows, :] = offset[k] + time_step * v
                out_ref[3 + k, rows, :] = v
                for j in range(3):
                    out_ref[6 + 3 * k + j, rows, :] = (-4.0 * v) * offset[j]
        return carry

    lax.fori_loop(0, blocks // SPAN, step, 0)


def grid_kernel(tiles_ref, lists_ref, counts_ref, ends_ref, up_ref, mid_ref, down_ref,
                before_ref, after_ref, off_ref, mass_ref, cell_ref,
                settled_ref, cols_ref, rec_ref, speed_ref, *, row, margin):
    total = settled_ref.shape[0]
    side = before_ref.shape[0]
    inner = side - row
    rid = lax.broadcasted_iota(jnp.int32, (1, 8, LANES), 1)
    pull = jnp.zeros((1, 8, LANES), jnp.float32)
    for k in range(3):
        pull = jnp.where(rid % 4 == k, time_step * gravity_pull[k], pull)

    def speed_of(x):
        mass = jnp.where(rid < 4, x[:, 3:4, :], x[:, 7:8, :])
        return x / jnp.maximum(mass, 1.0) + pull

    chunk = 8
    keep_first = 1.0 - ends_ref[0].astype(jnp.float32)
    keep_last = 1.0 - ends_ref[1].astype(jnp.float32)
    far = row + total - side

    def middle(i, carry):
        at = i * chunk
        speed_ref[pl.ds(row + side + at, chunk)] = speed_of(mid_ref[pl.ds(at, chunk)])
        return carry

    lax.fori_loop(0, mid_ref.shape[0] // chunk, middle, 0)

    def outer(i, carry):
        at = i * chunk
        speed_ref[pl.ds(at, chunk)] = speed_of(before_ref[pl.ds(at, chunk)]) * keep_first
        speed_ref[pl.ds(side + at, chunk)] = speed_of(up_ref[pl.ds(inner + at, chunk)])
        speed_ref[pl.ds(far + at, chunk)] = speed_of(down_ref[pl.ds(at, chunk)])
        speed_ref[pl.ds(row + total + at, chunk)] = (
            speed_of(after_ref[pl.ds(inner + at, chunk)]) * keep_last)
        return carry

    lax.fori_loop(0, row // chunk, outer, 0)

    def seam(i, carry):
        at = i * chunk
        x = speed_of(up_ref[pl.ds(at, chunk)] + before_ref[pl.ds(row + at, chunk)])
        speed_ref[pl.ds(row + at, chunk)] = x * jnp.where(at < margin * row, keep_first, 1.0)
        y = speed_of(down_ref[pl.ds(row + at, chunk)] + after_ref[pl.ds(at, chunk)])
        past = at >= inner - margin * row
        speed_ref[pl.ds(far + row + at, chunk)] = y * jnp.where(past, keep_last, 1.0)
        return carry

    lax.fori_loop(0, inner // chunk, seam, 0)

    def smooth(i, carry):
        at = i * chunk
        s = speed_ref[pl.ds(row + at, chunk)]
        settled_ref[pl.ds(at, chunk)] = s + viscosity * (
            speed_ref[pl.ds(2 * row + at, chunk)] + speed_ref[pl.ds(at, chunk)] - 2.0 * s)
        return carry

    lax.fori_loop(0, total // chunk, smooth, 0)

    planes = cols_ref.shape[1]
    flat = settled_ref.reshape(total * 8, LANES)

    def column(tc, carry):
        for group in range(planes // 8):
            for h in range(2):
                for k in range(3):
                    start = (margin + group * 8) * row * 8 + tc * 8 + h * 4 + k
                    x = flat[pl.ds(start, 8, stride=row * 8), :]
                    at = pl.multiple_of(tc * TILE + h * LANES, LANES)
                    cols_ref[k, group * 8:group * 8 + 8, pl.ds(at, LANES)] = x
        return carry

    lax.fori_loop(0, row, column, 0)

    slots = lists_ref.shape[1]

    def record(i, carry):
        for way in range(2):
            b = lists_ref[way, i]
            keep = jnp.where(i < counts_ref[way], 1.0, 0.0)
            c = cell_ref[pl.ds(b, 1), :]
            tile = settled_ref[tiles_ref[b]]
            lane = jnp.broadcast_to(c & (LANES - 1), (8, LANES))
            g = jnp.take_along_axis(tile, lane, axis=1)
            v = jnp.where(c >= LANES, g[4:7], g[0:3])
            at = way * slots + i
            for k in range(3):
                o = off_ref[k, pl.ds(b, 1), :]
                rec_ref[at, k:k + 1, :] = (o + time_step * v[k:k + 1]) * keep
                rec_ref[at, pl.ds(6 + k, 3, stride=3), :] = ((-4.0 * v) * o) * keep
            rec_ref[at, 3:6, :] = v * keep
            rec_ref[at, 15:16, :] = mass_ref[pl.ds(b, 1), :] * keep
        return carry

    lax.fori_loop(0, slots, record, 0)


def body(offsets, velocity, affine, particle_mass, cell_in_tile, block_tile, live_blocks,
         send_lists, send_counts):
    axes = ("slab", "deal")
    slabs, deals = lax.axis_size("slab"), lax.axis_size("deal")
    count = slabs * deals
    slab, deal = lax.axis_index("slab"), lax.axis_index("deal")
    nb = offsets.shape[0]
    row = PLANE // TILE
    planes = PX // deals
    share = planes * row
    margin = -(-max(share // 16, 1) // row)
    total = (planes + 2 * margin) * row
    side = (2 * margin + 1) * row
    f32 = jnp.float32

    tiles = block_tile - (deal * share - margin * row)
    live = live_blocks[0, 0]
    low = jnp.minimum(jnp.sum((tiles < side).astype(jnp.int32)), live)
    high = jnp.minimum(jnp.sum((tiles < total - side).astype(jnp.int32)), live)
    marks = jnp.stack([low, high, live])
    offsets, velocity, affine = (jnp.transpose(x, (1, 0, 2)) for x in (offsets, velocity, affine))
    blocks = 128 if nb % 128 == 0 else nb
    steps = nb // blocks
    params = pltpu.CompilerParams(vmem_limit_bytes=VMEM_LIMIT)
    smem = pl.BlockSpec(memory_space=pltpu.SMEM)
    vmem = pl.BlockSpec(memory_space=pltpu.VMEM)

    def edge_chunk(i, marks_ref):
        held = jnp.maximum(lax.div(marks_ref[0] + blocks - 1, blocks) - 1, 0)
        used = (i * blocks < marks_ref[0]) | ((i + 1) * blocks > marks_ref[1])
        return jnp.where(used, i, held)

    def middle_chunk(i, marks_ref):
        first = jnp.minimum(lax.div(marks_ref[0], blocks), steps - 1)
        last = jnp.maximum(lax.div(marks_ref[1] + blocks - 1, blocks) - 1, first)
        return jnp.clip(i, first, last)

    def deposit(kernel, chunk, sizes, shift, name):
        def part(*lead):
            return pl.BlockSpec(lead + (blocks, LANES),
                                lambda i, m, t: (0,) * len(lead) + (chunk(i, m), 0))

        return pl.pallas_call(
            functools.partial(kernel, blocks=blocks, shift=shift),
            grid_spec=pltpu.PrefetchScalarGridSpec(
                num_scalar_prefetch=2,
                grid=(steps,),
                in_specs=[part(3), part(3), part(9), part(), part()],
                out_specs=[pl.BlockSpec((n, 8, LANES), lambda i, m, t: (0, 0, 0)) for n in sizes],
                scratch_shapes=[pltpu.VMEM((SPAN * 16, LANES), f32)],
            ),
            out_shape=[jax.ShapeDtypeStruct((n, 8, LANES), f32) for n in sizes],
            compiler_params=params,
            cost_estimate=pl.CostEstimate(flops=nb * 16 * LANES * LANES, transcendentals=0,
                                          bytes_accessed=nb * 17 * LANES * 4),
            name=name,
        )(marks, tiles, offsets, velocity, affine, particle_mass, cell_in_tile)

    up, down = deposit(edge_kernel, edge_chunk, (side, side), total - side, "deposit_edges")
    before = lax.ppermute(down, axes, [(i, i + 1) for i in range(count - 1)])
    after = lax.ppermute(up, axes, [(i + 1, i) for i in range(count - 1)])
    mid, = deposit(middle_kernel, middle_chunk, (total - 2 * side,), side, "deposit_middle")

    place = slab * deals + deal
    ends = jnp.stack([place == 0, place == count - 1]).astype(jnp.int32)
    mig = send_lists.shape[-1]
    settled, cols, records = pl.pallas_call(
        functools.partial(grid_kernel, row=row, margin=margin),
        in_specs=[smem] * 4 + [vmem] * 8,
        out_specs=[vmem] * 3,
        out_shape=[jax.ShapeDtypeStruct((total, 8, LANES), f32),
                   jax.ShapeDtypeStruct((3, planes, PLANE), f32),
                   jax.ShapeDtypeStruct((2 * mig, 16, LANES), f32)],
        scratch_shapes=[pltpu.VMEM((total + 2 * row, 8, LANES), f32)],
        compiler_params=params,
        name="grid_step",
    )(tiles, send_lists[0, 0], send_counts.reshape(2), ends, up, mid, down, before, after,
      offsets, particle_mass, cell_in_tile)

    from_left = lax.ppermute(records[:mig], "slab", [(i, i + 1) for i in range(slabs - 1)])
    from_right = lax.ppermute(records[mig:], "slab", [(i + 1, i) for i in range(slabs - 1)])

    width = PLANE // deals
    pieces = [lax.dynamic_slice_in_dim(cols, deal * width, width, axis=2)]
    for k in range(1, deals):
        chosen = lax.dynamic_slice_in_dim(cols, ((deal + k) % deals) * width, width, axis=2)
        pieces.append(lax.ppermute(chosen, "deal", [(i, (i + k) % deals) for i in range(deals)]))

    state = pl.pallas_call(
        functools.partial(update_kernel, blocks=blocks),
        grid=(steps,),
        in_specs=[smem, pl.BlockSpec((3, blocks, LANES), lambda i: (0, i, 0)),
                  pl.BlockSpec((blocks, LANES), lambda i: (i, 0)),
                  pl.BlockSpec((total, 8, LANES), lambda i: (0, 0, 0))],
        out_specs=pl.BlockSpec((15, blocks, LANES), lambda i: (0, i, 0)),
        out_shape=jax.ShapeDtypeStruct((15, nb, LANES), f32),
        scratch_shapes=[pltpu.VMEM((SPAN * 8, LANES), f32)],
        compiler_params=params,
        cost_estimate=pl.CostEstimate(flops=nb * 15 * LANES * 4,
                                      bytes_accessed=nb * 20 * LANES * 4, transcendentals=0),
        name="update",
    )(tiles, offsets, cell_in_tile, settled)
    state = jnp.transpose(state, (1, 0, 2))

    arrivals = jnp.stack([from_left, from_right], axis=0)[None, None]
    grid = jnp.zeros((3, PX, width), f32)
    for k in range(deals):
        grid = lax.dynamic_update_slice_in_dim(
            grid, pieces[k], ((deal - k) % deals) * planes, axis=1)
    return state, arrivals, grid


def solution(mesh):
    placed = (
        P(("slab", "deal"), None, None),
        P(("slab", "deal"), None, None),
        P(("slab", "deal"), None, None),
        P(("slab", "deal"), None),
        P(("slab", "deal"), None),
        P(("slab", "deal")),
        P("slab", "deal"),
        P("slab", "deal", None, None),
        P("slab", "deal", None),
    )
    return jax.shard_map(
        body,
        mesh=mesh,
        in_specs=placed,
        out_specs=(
            P(("slab", "deal"), None, None),
            P("slab", "deal", None, None, None, None),
            P(None, "slab", "deal"),
        ),
        check_vma=False,
    )
```

time: 121 us -> 83.7 us (0.69)
  the two profiles are of different devices: /device:TPU:1 before, /device:TPU:26 now
where the time goes in v2:
time: 83.7 us; the launch traced here: 83.4 us
  Pallas kernels  34.8 us (42%)
  starting transfers between devices  19.3 us (23%)
  local copies, waits for them, and re-layouts  17.9 us (21%)
  waiting for transfers between devices  5.4 us (6%)
  other arithmetic  3.11 us (4%)
  between operations  2.9 us (3%)
    pallas_call x2, Pallas kernels, deposit(): pl.pallas_call(functools.partial(kernel, blocks=blocks, shift=shift), gri...  21 us
    unnamed x34, local copies, waits for them, and re-layouts  14.9 us
    pallas_call x1, Pallas kernels, body(): pl.pallas_call(functools.partial(update_kernel, blocks=blocks), grid=(ste...  8.12 us
    ppermute x1, starting transfers between devices, body(): before = lax.ppermute(down, axes, [(i, i + 1) for i in range(count - 1)])  7.42 us
    pallas_call x1, Pallas kernels, body(): pl.pallas_call(functools.partial(grid_kernel, row=row, margin=margin), in...  5.7 us
    ppermute x3, waiting for transfers between devices, body(): lax.ppermute(chosen, 'deal', [(i, (i + k) % deals) for i in range(deals)])  5.39 us
    ppermute x3, starting transfers between devices, body(): lax.ppermute(chosen, 'deal', [(i, (i + k) % deals) for i in range(deals)])  4.42 us
    ppermute x1, starting transfers between devices, body(): lax.ppermute(records[mig:], 'slab', [(i + 1, i) for i in range(slabs - 1)])  3.64 us
  transfers between devices with their start and end apart: 7, of which 1 were waited for; matrix products, arithmetic and copies ran while one was open for 5% of the time, Pallas kernels for 28%

profile of v2, /device:TPU:26, one launch (start us, length us, event | category | flops | bytes accessed | tf_op | source)
XLA Modules:
  0.0 83.4 jit_solution(6062038554172436956)
XLA Ops:
  1.3 1.3 %convert_reduce_fusion.1 = (s32[]{:T(128)}, s32[]{:T(128)}, s32[1024]{0:T(1024)S(1)}) fusion(s32[1024]{0:T(1024)} %param.14, s32[]{:T(128)S(6)} %sub.18), kind=kLoop, calls=%fused_computation.3 | loop fusion | flops 7166 | bytes 8204 | tf_op jit(solution)/shard_map/reduce_sum | solution.py:242
  4.0 1.4 %copy-done = f32[1024,3,128]{2,0,1:T(8,128)S(1)} copy-done((f32[1024,3,128]{2,0,1:T(8,128)S(1)}, f32[1024,3,128]{2,0,1:T(8,128)}, u32[]{:S(2)}) %copy-start) | copy-done | bytes 1572888
  5.4 2.3 %copy-done.2 = f32[1024,9,128]{2,0,1:T(8,128)S(1)} copy-done((f32[1024,9,128]{2,0,1:T(8,128)S(1)}, f32[1024,9,128]{2,0,1:T(8,128)}, u32[]{:S(2)}) %copy-start.2) | copy-done | bytes 4718616
  7.7 1.0 %copy-done.4 = s32[1024,128]{1,0:T(8,128)S(1)} copy-done((s32[1024,128]{1,0:T(8,128)S(1)}, s32[1024,128]{1,0:T(8,128)}, u32[]{:S(2)}) %copy-start.4) | copy-done | bytes 524312
  8.8 1.4 %copy-done.6 = f32[1024,3,128]{2,0,1:T(8,128)S(1)} copy-done((f32[1024,3,128]{2,0,1:T(8,128)S(1)}, f32[1024,3,128]{2,0,1:T(8,128)}, u32[]{:S(2)}) %copy-start.6) | copy-done | bytes 1572888
  10.2 1.0 %copy-done.8 = f32[1024,128]{1,0:T(8,128)S(1)} copy-done((f32[1024,128]{1,0:T(8,128)S(1)}, f32[1024,128]{1,0:T(8,128)}, u32[]{:S(2)}) %copy-start.8) | copy-done | bytes 524312
  11.2 5.7 %deposit_edges.1 = (f32[96,8,128]{2,1,0:T(8,128)S(1)}, f32[96,8,128]{2,1,0:T(8,128)S(1)}) custom-call(s32[3]{0:T(128)S(1)} %pad_add_fusion.marks_ref, s32[1024]{0:T(1024)S(1)} %get-tuple-element.15.tiles_ref, f32[3,1024,128]{2,1,0:T(8,128)S(1)} %bitcast.19, f32[3,1024,128]{2,1,0:T(8,128)S(1)} %bitcast.25, f32[9,1024,128]{2,1,0:T(8,128)S(1)} %bitcast.23, ...), custom_call_target="tpu_custom_call" | custom-call | flops 268435456 | bytes 8912896 | tf_op jit(solution)/shard_map/deposit_edges/pallas_call | solution.py:267
  16.9 1.9 %collective-permute-start.1 = (f32[96,8,128]{2,1,0:T(8,128)S(1)}, f32[96,8,128]{2,1,0:T(8,128)}, u32[]{:S(2)}, u32[]{:S(2)}) collective-permute-start(f32[96,8,128]{2,1,0:T(8,128)S(1)} %get-tuple-element.8.up_ref), channel_id=1, source_target_pairs={{1,0},{2,1},{3,2},{4,3},{5,4},{6,5},{7,6},{8,7},{9,8},{10,9},{11,1... | collective-permute-start | bytes 1179656 | tf_op jit(solution)/shard_map/ppermute | solution.py:285
  18.9 7.4 %collective-permute-start = (f32[96,8,128]{2,1,0:T(8,128)S(1)}, f32[96,8,128]{2,1,0:T(8,128)}, u32[]{:S(2)}, u32[]{:S(2)}) collective-permute-start(f32[96,8,128]{2,1,0:T(8,128)S(1)} %get-tuple-element.9.down_ref), channel_id=1, source_target_pairs={{0,1},{1,2},{2,3},{3,4},{4,5},{5,6},{6,7},{7,8},{8,9},{9,10},{10,1... | collective-permute-start | bytes 1179656 | tf_op jit(solution)/shard_map/ppermute | solution.py:284
  26.4 2.3 %copy-done.3 = f32[1024,9,128]{2,0,1:T(8,128)S(1)} copy-done((f32[1024,9,128]{2,0,1:T(8,128)S(1)}, f32[1024,9,128]{2,0,1:T(8,128)}, u32[]{:S(2)}) %copy-start.3) | copy-done | bytes 4718616
  28.7 1.4 %copy-done.7 = f32[1024,3,128]{2,0,1:T(8,128)S(1)} copy-done((f32[1024,3,128]{2,0,1:T(8,128)S(1)}, f32[1024,3,128]{2,0,1:T(8,128)}, u32[]{:S(2)}) %copy-start.7) | copy-done | bytes 1572888
  30.1 15.3 %deposit_middle.1.mid_ref = f32[384,8,128]{2,1,0:T(8,128)S(1)} custom-call(s32[3]{0:T(128)S(1)} %pad_add_fusion.marks_ref, s32[1024]{0:T(1024)S(1)} %get-tuple-element.15.tiles_ref, f32[3,1024,128]{2,1,0:T(8,128)S(1)} %bitcast.20, f32[3,1024,128]{2,1,0:T(8,128)S(1)} %bitcast.26, f32[9,1024,128]{2,1,0:T(8,128)S(1)} %bitcast.24, f32[1024,128]{1,0:T(8,128)S(1)} %copy-done.9, ...), custom_call_target="tpu_custom_call" | custom-call | flops 268435456 | bytes 8912896 | tf_op jit(solution)/shard_map/deposit_middle/pallas_call | solution.py:267
  45.5 5.7 %grid_step.1 = (f32[576,8,128]{2,1,0:T(8,128)S(1)}, f32[3,16,8192]{2,1,0:T(8,128)S(1)}, f32[32,16,128]{2,1,0:T(8,128)S(1)}) custom-call(s32[1024]{0:T(1024)S(1)} %get-tuple-element.15.tiles_ref, s32[2,16]{1,0:T(2,128)S(1)} %bitcast.27, s32[2]{0:T(128)S(1)} %bitcast.28, s32[2]{0:T(128)S(1)} %add_convert_fusion.ends_ref, ...), custom_call_target="tpu_custom_call" | custom-call | tf_op jit(solution)/shard_map/grid_step/pallas_call | solution.py:291
  51.5 1.1 %copy-done.10 = f32[576,8,128]{2,1,0:T(8,128)} copy-done((f32[576,8,128]{2,1,0:T(8,128)}, f32[576,8,128]{2,1,0:T(8,128)S(1)}, u32[]{:S(2)}) %copy-start.10) | copy-done | bytes 2359320
  52.6 3.4 %collective-permute-start.4 = (f32[3,16,2048]{2,1,0:T(8,128)S(1)}, f32[3,16,2048]{2,1,0:T(8,128)}, u32[]{:S(2)}, u32[]{:S(2)}) collective-permute-start(f32[3,16,2048]{2,1,0:T(8,128)S(1)} %get-tuple-element.18), channel_id=1, source_target_pairs={{0,1},{1,2},{2,3},{3,0},{4,5},{5,6},{6,7},{7,4},{8,9},{9,10},{10,1... | collective-permute-start | bytes 1179656 | tf_op jit(solution)/shard_map/ppermute | solution.py:311
  56.7 1.9 %collective-permute-start.2 = (f32[16,16,128]{2,1,0:T(8,128)}, f32[16,16,128]{2,1,0:T(8,128)S(1)}, u32[]{:S(2)}, u32[]{:S(2)}) collective-permute-start(f32[16,16,128]{2,1,0:T(8,128)} %get-tuple-element.20), channel_id=1, source_target_pairs={{0,4},{4,8},{8,12},{12,16},{16,20},{20,24},{24,28},{1,5},{5,9},{9,... | collective-permute-start | bytes 393224 | tf_op jit(solution)/shard_map/ppermute | solution.py:304
  58.6 3.6 %collective-permute-start.3 = (f32[16,16,128]{2,1,0:T(8,128)S(1)}, f32[16,16,128]{2,1,0:T(8,128)}, u32[]{:S(2)}, u32[]{:S(2)}) collective-permute-start(f32[16,16,128]{2,1,0:T(8,128)S(1)} %get-tuple-element.21), channel_id=1, source_target_pairs={{4,0},{8,4},{12,8},{16,12},{20,16},{24,20},{28,24},{5,1},{9,5},{13... | collective-permute-start | bytes 393224 | tf_op jit(solution)/shard_map/ppermute | solution.py:305
  63.4 1.7 %copy-done.11 = f32[576,8,128]{2,1,0:T(8,128)S(1)} copy-done((f32[576,8,128]{2,1,0:T(8,128)S(1)}, f32[576,8,128]{2,1,0:T(8,128)}, u32[]{:S(2)}) %copy-start.11) | copy-done | bytes 2359320
  65.0 8.1 %update.1 = f32[15,1024,128]{2,1,0:T(8,128)} custom-call(s32[1024]{0:T(1024)S(1)} %get-tuple-element.15.tiles_ref, f32[3,1024,128]{2,1,0:T(8,128)S(1)} %bitcast.22, s32[1024,128]{1,0:T(8,128)S(1)} %copy-done.5, f32[576,8,128]{2,1,0:T(8,128)S(1)} %copy-done.11), custom_call_target="tpu_custom_call" | custom-call | flops 7864320 | bytes 10485760 | tf_op jit(solution)/shard_map/update/pallas_call | solution.py:313
  73.2 1.6 %maximum_bitcast_fusion = f32[1,1,2,16,16,128]{5,4,3,2,1,0:T(8,128)} fusion(f32[1,16,16,128]{3,2,1,0:T(8,128)} %bitcast.13, f32[1,16,16,128]{3,2,1,0:T(8,128)S(1)} %bitcast.30), kind=kLoop, calls=%fused_computation.1 | loop fusion | flops 65536 | bytes 524288 | tf_op jit(solution)/shard_map/broadcast_in_dim | solution.py:329
  74.8 1.0 %constant_dynamic-update-slice_fusion.2 = f32[3,64,2048]{2,1,0:T(8,128)S(1)} fusion(f32[3,64,2048]{2,1,0:T(8,128)S(1)} %copy-done.15, f32[3,16,2048]{2,1,0:T(8,128)} %collective-permute-done.4, s32[]{:T(128)S(6)} %select_n.61), kind=kLoop, calls=%fused_computation.8 | loop fusion | bytes 786436 | tf_op jit(solution)/shard_map/dynamic_update_slice | solution.py:332
  75.8 5.4 %collective-permute-done.5 = f32[3,16,2048]{2,1,0:T(8,128)} collective-permute-done((f32[3,16,2048]{2,1,0:T(8,128)S(1)}, f32[3,16,2048]{2,1,0:T(8,128)}, u32[]{:S(2)}, u32[]{:S(2)}) %collective-permute-start.5) | collective-permute-done | bytes 393248 | tf_op jit(solution)/shard_map/ppermute | solution.py:311
  81.2 1.0 %constant_dynamic-update-slice_fusion.1 = f32[3,64,2048]{2,1,0:T(8,128)S(1)} fusion(f32[3,64,2048]{2,1,0:T(8,128)S(1)} %constant_dynamic-update-slice_fusion.2, f32[3,16,2048]{2,1,0:T(8,128)} %collective-permute-done.5, s32[]{:T(128)S(6)} %select_n.65), kind=kLoop, calls=%fused_computation.6 | loop fusion | bytes 786436 | tf_op jit(solution)/shard_map/dynamic_update_slice | solution.py:332
  82.3 1.1 %copy-done.16 = f32[3,64,2048]{2,1,0:T(8,128)} copy-done((f32[3,64,2048]{2,1,0:T(8,128)}, f32[3,64,2048]{2,1,0:T(8,128)S(1)}, u32[]{:S(2)}) %copy-start.16) | copy-done | bytes 1572888
  (38 shorter events, 2.3 us)
Async XLA Ops:
  4.0 1.4 %copy-start = (f32[1024,3,128]{2,0,1:T(8,128)S(1)}, f32[1024,3,128]{2,0,1:T(8,128)}, u32[]{:S(2)}) copy-start(f32[1024,3,128]{2,0,1:T(8,128)} %param.9) | copy-start | bytes 4718596
  5.4 2.3 %copy-start.2 = (f32[1024,9,128]{2,0,1:T(8,128)S(1)}, f32[1024,9,128]{2,0,1:T(8,128)}, u32[]{:S(2)}) copy-start(f32[1024,9,128]{2,0,1:T(8,128)} %param.11) | copy-start | bytes 14155780
  7.7 1.0 %copy-start.4 = (s32[1024,128]{1,0:T(8,128)S(1)}, s32[1024,128]{1,0:T(8,128)}, u32[]{:S(2)}) copy-start(s32[1024,128]{1,0:T(8,128)} %cell_ref.3) | copy-start | bytes 1572868
  8.8 1.4 %copy-start.6 = (f32[1024,3,128]{2,0,1:T(8,128)S(1)}, f32[1024,3,128]{2,0,1:T(8,128)}, u32[]{:S(2)}) copy-start(f32[1024,3,128]{2,0,1:T(8,128)} %param.10) | copy-start | bytes 4718596
  10.2 1.0 %copy-start.8 = (f32[1024,128]{1,0:T(8,128)S(1)}, f32[1024,128]{1,0:T(8,128)}, u32[]{:S(2)}) copy-start(f32[1024,128]{1,0:T(8,128)} %mass_ref.1) | copy-start | bytes 1572868
  11.2 15.1 %copy-start.1 = (f32[1024,3,128]{2,0,1:T(8,128)S(1)}, f32[1024,3,128]{2,0,1:T(8,128)}, u32[]{:S(2)}) copy-start(f32[1024,3,128]{2,0,1:T(8,128)} %param.9) | copy-start | bytes 4718596
  11.2 15.1 %copy-start.5 = (s32[1024,128]{1,0:T(8,128)S(1)}, s32[1024,128]{1,0:T(8,128)}, u32[]{:S(2)}) copy-start(s32[1024,128]{1,0:T(8,128)} %cell_ref.3) | copy-start | bytes 1572868
  11.2 15.1 %copy-start.9 = (f32[1024,128]{1,0:T(8,128)S(1)}, f32[1024,128]{1,0:T(8,128)}, u32[]{:S(2)}) copy-start(f32[1024,128]{1,0:T(8,128)} %mass_ref.1) | copy-start | bytes 1572868
  16.9 28.6 %collective-permute-start.1 = (f32[96,8,128]{2,1,0:T(8,128)S(1)}, f32[96,8,128]{2,1,0:T(8,128)}, u32[]{:S(2)}, u32[]{:S(2)}) collective-permute-start(f32[96,8,128]{2,1,0:T(8,128)S(1)} %get-tuple-element.8.up_ref), channel_id=1, source_target_pairs={{1,0},{2,1},{3,2},{4,3},{5,4},{6,5},{7,6},{8,7},{9,8},{10,9},{11,1... | collective-permute-start | bytes 1179656 | tf_op jit(solution)/shard_map/ppermute | solution.py:285
  18.9 26.6 %collective-permute-start = (f32[96,8,128]{2,1,0:T(8,128)S(1)}, f32[96,8,128]{2,1,0:T(8,128)}, u32[]{:S(2)}, u32[]{:S(2)}) collective-permute-start(f32[96,8,128]{2,1,0:T(8,128)S(1)} %get-tuple-element.9.down_ref), channel_id=1, source_target_pairs={{0,1},{1,2},{2,3},{3,4},{4,5},{5,6},{6,7},{7,8},{8,9},{9,10},{10,1... | collective-permute-start | bytes 1179656 | tf_op jit(solution)/shard_map/ppermute | solution.py:284
  26.4 2.3 %copy-start.3 = (f32[1024,9,128]{2,0,1:T(8,128)S(1)}, f32[1024,9,128]{2,0,1:T(8,128)}, u32[]{:S(2)}) copy-start(f32[1024,9,128]{2,0,1:T(8,128)} %param.11) | copy-start | bytes 14155780
  28.7 1.4 %copy-start.7 = (f32[1024,3,128]{2,0,1:T(8,128)S(1)}, f32[1024,3,128]{2,0,1:T(8,128)}, u32[]{:S(2)}) copy-start(f32[1024,3,128]{2,0,1:T(8,128)} %param.10) | copy-start | bytes 4718596
  30.1 15.4 %copy-start.12 = (s32[1,1,2,16]{3,2,1,0:T(2,128)S(1)}, s32[1,1,2,16]{3,2,1,0:T(2,128)}, u32[]{:S(2)}) copy-start(s32[1,1,2,16]{3,2,1,0:T(2,128)} %param.16) | copy-start | bytes 388
  30.1 15.4 %copy-start.13 = (s32[1,1,2]{2,1,0:T(1,128)S(1)}, s32[1,1,2]{2,1,0:T(1,128)}, u32[]{:S(2)}) copy-start(s32[1,1,2]{2,1,0:T(1,128)} %param.17) | copy-start | bytes 28
  51.2 1.4 %copy-start.10 = (f32[576,8,128]{2,1,0:T(8,128)}, f32[576,8,128]{2,1,0:T(8,128)S(1)}, u32[]{:S(2)}) copy-start(f32[576,8,128]{2,1,0:T(8,128)S(1)} %get-tuple-element.10.settled_ref) | copy-start | bytes 7077892
  52.6 4.0 %copy-start.14 = (f32[3,64,2048]{2,1,0:T(8,128)}, f32[3,64,2048]{2,1,0:T(8,128)S(1)}, u32[]{:S(2)}) copy-start(f32[3,64,2048]{2,1,0:T(8,128)S(1)} %get-tuple-element.19) | copy-start | bytes 4718596
  52.6 22.2 %collective-permute-start.4 = (f32[3,16,2048]{2,1,0:T(8,128)S(1)}, f32[3,16,2048]{2,1,0:T(8,128)}, u32[]{:S(2)}, u32[]{:S(2)}) collective-permute-start(f32[3,16,2048]{2,1,0:T(8,128)S(1)} %get-tuple-element.18), channel_id=1, source_target_pairs={{0,1},{1,2},{2,3},{3,0},{4,5},{5,6},{6,7},{7,4},{8,9},{9,10},{10,1... | collective-permute-start | bytes 1179656 | tf_op jit(solution)/shard_map/ppermute | solution.py:311
  56.7 16.5 %collective-permute-start.2 = (f32[16,16,128]{2,1,0:T(8,128)}, f32[16,16,128]{2,1,0:T(8,128)S(1)}, u32[]{:S(2)}, u32[]{:S(2)}) collective-permute-start(f32[16,16,128]{2,1,0:T(8,128)} %get-tuple-element.20), channel_id=1, source_target_pairs={{0,4},{4,8},{8,12},{12,16},{16,20},{20,24},{24,28},{1,5},{5,9},{9,... | collective-permute-start | bytes 393224 | tf_op jit(solution)/shard_map/ppermute | solution.py:304
  58.6 14.6 %collective-permute-start.3 = (f32[16,16,128]{2,1,0:T(8,128)S(1)}, f32[16,16,128]{2,1,0:T(8,128)}, u32[]{:S(2)}, u32[]{:S(2)}) collective-permute-start(f32[16,16,128]{2,1,0:T(8,128)S(1)} %get-tuple-element.21), channel_id=1, source_target_pairs={{4,0},{8,4},{12,8},{16,12},{20,16},{24,20},{28,24},{5,1},{9,5},{13... | collective-permute-start | bytes 393224 | tf_op jit(solution)/shard_map/ppermute | solution.py:305
  62.2 19.0 %collective-permute-start.5 = (f32[3,16,2048]{2,1,0:T(8,128)S(1)}, f32[3,16,2048]{2,1,0:T(8,128)}, u32[]{:S(2)}, u32[]{:S(2)}) collective-permute-start(f32[3,16,2048]{2,1,0:T(8,128)S(1)} %get-tuple-element.17), channel_id=1, source_target_pairs={{0,2},{1,3},{2,0},{3,1},{4,6},{5,7},{6,4},{7,5},{8,10},{9,11},{10,... | collective-permute-start | bytes 1179656 | tf_op jit(solution)/shard_map/ppermute | solution.py:311
  62.4 19.9 %collective-permute-start.6 = (f32[3,16,2048]{2,1,0:T(8,128)S(1)}, f32[3,16,2048]{2,1,0:T(8,128)S(1)}, u32[]{:S(2)}, u32[]{:S(2)}) collective-permute-start(f32[3,16,2048]{2,1,0:T(8,128)S(1)} %get-tuple-element.16), channel_id=1, source_target_pairs={{0,3},{1,0},{2,1},{3,2},{4,7},{5,4},{6,5},{7,6},{8,11},{9,8},{10,9... | collective-permute-start | bytes 1179656 | tf_op jit(solution)/shard_map/ppermute | solution.py:311
  63.4 1.7 %copy-start.11 = (f32[576,8,128]{2,1,0:T(8,128)S(1)}, f32[576,8,128]{2,1,0:T(8,128)}, u32[]{:S(2)}) copy-start(f32[576,8,128]{2,1,0:T(8,128)} %copy-done.10) | copy-start | bytes 7077892
  65.0 9.8 %copy-start.15 = (f32[3,64,2048]{2,1,0:T(8,128)S(1)}, f32[3,64,2048]{2,1,0:T(8,128)}, u32[]{:S(2)}) copy-start(f32[3,64,2048]{2,1,0:T(8,128)} %copy-done.14) | copy-start | bytes 4718596
  82.3 1.1 %copy-start.16 = (f32[3,64,2048]{2,1,0:T(8,128)}, f32[3,64,2048]{2,1,0:T(8,128)S(1)}, u32[]{:S(2)}) copy-start(f32[3,64,2048]{2,1,0:T(8,128)S(1)} %constant_dynamic-update-slice_fusion) | copy-start | bytes 4718596

commit v3 on v2

--- a/solution.py
+++ b/solution.py
@@ -17,7 +17,7 @@
 viscosity = 0.2
 gravity_pull = (3.0, 0.0, -5.0)
 
-VMEM_LIMIT = 40 * 1024 * 1024
+VMEM_LIMIT = 60 * 1024 * 1024
 
 
 def deposit_span(at, first, start, stop, ins, out_ref, shift, tiles_ref, parts_ref):
@@ -128,7 +128,9 @@
 
 def grid_kernel(tiles_ref, lists_ref, counts_ref, ends_ref, up_ref, mid_ref, down_ref,
                 before_ref, after_ref, off_ref, mass_ref, cell_ref,
-                settled_ref, cols_ref, rec_ref, speed_ref, *, row, margin):
+                settled_ref, *refs, row, margin, deals):
+    *piece_refs, rec_down_ref, rec_up_ref, speed_ref = refs
+    rec_refs = (rec_down_ref, rec_up_ref)
     total = settled_ref.shape[0]
     side = before_ref.shape[0]
     inner = side - row
@@ -184,20 +186,24 @@
 
     lax.fori_loop(0, total // chunk, smooth, 0)
 
-    planes = cols_ref.shape[1]
     flat = settled_ref.reshape(total * 8, LANES)
-
-    def column(tc, carry):
-        for group in range(planes // 8):
-            for h in range(2):
-                for k in range(3):
-                    start = (margin + group * 8) * row * 8 + tc * 8 + h * 4 + k
-                    x = flat[pl.ds(start, 8, stride=row * 8), :]
-                    at = pl.multiple_of(tc * TILE + h * LANES, LANES)
-                    cols_ref[k, group * 8:group * 8 + 8, pl.ds(at, LANES)] = x
-        return carry
-
-    lax.fori_loop(0, row, column, 0)
+    planes = piece_refs[0].shape[1]
+    across = row // deals
+    for turn in range(deals):
+        piece_ref = piece_refs[turn]
+        corner = lax.rem(ends_ref[2] + turn, deals) * across
+
+        def column(tc, carry, piece_ref=piece_ref, corner=corner):
+            for group in range(planes // 8):
+                for h in range(2):
+                    for k in range(3):
+                        start = (margin + group * 8) * row * 8 + (corner + tc) * 8 + h * 4 + k
+                        x = flat[pl.ds(start, 8, stride=row * 8), :]
+                        at = pl.multiple_of(tc * TILE + h * LANES, LANES)
+                        piece_ref[k, group * 8:group * 8 + 8, pl.ds(at, LANES)] = x
+            return carry
+
+        lax.fori_loop(0, across, column, 0)
 
     slots = lists_ref.shape[1]
 
@@ -210,16 +216,33 @@
             lane = jnp.broadcast_to(c & (LANES - 1), (8, LANES))
             g = jnp.take_along_axis(tile, lane, axis=1)
             v = jnp.where(c >= LANES, g[4:7], g[0:3])
-            at = way * slots + i
+            rec_ref = rec_refs[way]
             for k in range(3):
                 o = off_ref[k, pl.ds(b, 1), :]
-                rec_ref[at, k:k + 1, :] = (o + time_step * v[k:k + 1]) * keep
-                rec_ref[at, pl.ds(6 + k, 3, stride=3), :] = ((-4.0 * v) * o) * keep
-            rec_ref[at, 3:6, :] = v * keep
-            rec_ref[at, 15:16, :] = mass_ref[pl.ds(b, 1), :] * keep
+                rec_ref[i, k:k + 1, :] = (o + time_step * v[k:k + 1]) * keep
+                rec_ref[i, pl.ds(6 + k, 3, stride=3), :] = ((-4.0 * v) * o) * keep
+            rec_ref[i, 3:6, :] = v * keep
+            rec_ref[i, 15:16, :] = mass_ref[pl.ds(b, 1), :] * keep
         return carry
 
     lax.fori_loop(0, slots, record, 0)
+
+
+def assemble_kernel(deal_ref, *refs, deals):
+    *piece_refs, left_ref, right_ref, grid_ref, arrivals_ref, sems = refs
+    planes = piece_refs[0].shape[1]
+    copies = []
+    for turn, piece_ref in enumerate(piece_refs):
+        slot = lax.rem(deal_ref[0] - turn + deals, deals)
+        rows = pl.ds(pl.multiple_of(slot * planes, 8), planes)
+        copies.append((piece_ref, grid_ref.at[:, rows, :]))
+    copies.append((left_ref, arrivals_ref.at[0]))
+    copies.append((right_ref, arrivals_ref.at[1]))
+    started = [pltpu.make_async_copy(a, b, sems.at[i]) for i, (a, b) in enumerate(copies)]
+    for c in started:
+        c.start()
+    for c in started:
+        c.wait()
 
 
 def body(offsets, velocity, affine, particle_mass, cell_in_tile, block_tile, live_blocks,
@@ -286,29 +309,28 @@
     mid, = deposit(middle_kernel, middle_chunk, (total - 2 * side,), side, "deposit_middle")
 
     place = slab * deals + deal
-    ends = jnp.stack([place == 0, place == count - 1]).astype(jnp.int32)
+    ends = jnp.stack([place == 0, place == count - 1, deal]).astype(jnp.int32)
     mig = send_lists.shape[-1]
-    settled, cols, records = pl.pallas_call(
-        functools.partial(grid_kernel, row=row, margin=margin),
+    width = PLANE // deals
+    outs = ([jax.ShapeDtypeStruct((total, 8, LANES), f32)]
+            + [jax.ShapeDtypeStruct((3, planes, width), f32)] * deals
+            + [jax.ShapeDtypeStruct((mig, 16, LANES), f32)] * 2)
+    settled, *pieces, leave_down, leave_up = pl.pallas_call(
+        functools.partial(grid_kernel, row=row, margin=margin, deals=deals),
         in_specs=[smem] * 4 + [vmem] * 8,
-        out_specs=[vmem] * 3,
-        out_shape=[jax.ShapeDtypeStruct((total, 8, LANES), f32),
-                   jax.ShapeDtypeStruct((3, planes, PLANE), f32),
-                   jax.ShapeDtypeStruct((2 * mig, 16, LANES), f32)],
+        out_specs=[vmem] * len(outs),
+        out_shape=outs,
         scratch_shapes=[pltpu.VMEM((total + 2 * row, 8, LANES), f32)],
         compiler_params=params,
         name="grid_step",
     )(tiles, send_lists[0, 0], send_counts.reshape(2), ends, up, mid, down, before, after,
       offsets, particle_mass, cell_in_tile)
 
-    from_left = lax.ppermute(records[:mig], "slab", [(i, i + 1) for i in range(slabs - 1)])
-    from_right = lax.ppermute(records[mig:], "slab", [(i + 1, i) for i in range(slabs - 1)])
-
-    width = PLANE // deals
-    pieces = [lax.dynamic_slice_in_dim(cols, deal * width, width, axis=2)]
     for k in range(1, deals):
-        chosen = lax.dynamic_slice_in_dim(cols, ((deal + k) % deals) * width, width, axis=2)
-        pieces.append(lax.ppermute(chosen, "deal", [(i, (i + k) % deals) for i in range(deals)]))
+        pairs = [(i, (i + k) % deals) for i in range(deals)]
+        pieces[k] = lax.ppermute(pieces[k], "deal", pairs)
+    from_left = lax.ppermute(leave_down, "slab", [(i, i + 1) for i in range(slabs - 1)])
+    from_right = lax.ppermute(leave_up, "slab", [(i + 1, i) for i in range(slabs - 1)])
 
     state = pl.pallas_call(
         functools.partial(update_kernel, blocks=blocks),
@@ -326,11 +348,18 @@
     )(tiles, offsets, cell_in_tile, settled)
     state = jnp.transpose(state, (1, 0, 2))
 
-    arrivals = jnp.stack([from_left, from_right], axis=0)[None, None]
-    grid = jnp.zeros((3, PX, width), f32)
-    for k in range(deals):
-        grid = lax.dynamic_update_slice_in_dim(
-            grid, pieces[k], ((deal - k) % deals) * planes, axis=1)
+    anywhere = pl.BlockSpec(memory_space=pl.ANY)
+    grid, arrivals = pl.pallas_call(
+        functools.partial(assemble_kernel, deals=deals),
+        in_specs=[smem] + [anywhere] * (deals + 2),
+        out_specs=[anywhere] * 2,
+        out_shape=[jax.ShapeDtypeStruct((3, PX, width), f32),
+                   jax.ShapeDtypeStruct((2, mig, 16, LANES), f32)],
+        scratch_shapes=[pltpu.SemaphoreType.DMA((deals + 2,))],
+        compiler_params=pltpu.CompilerParams(vmem_limit_bytes=VMEM_LIMIT // 4),
+        name="assemble",
+    )(ends[2:], *pieces, from_left, from_right)
+    arrivals = arrivals[None, None]
     return state, arrivals, grid
 
 

time: 83.7 us -> 76.2 us (0.910)
  the two profiles are of different devices: /device:TPU:26 before, /device:TPU:1 now
where the time goes in v3:
time: 76.2 us; the launch traced here: 75.2 us
  Pallas kernels  44.1 us (58%)
  starting transfers between devices  24.3 us (32%)
  other arithmetic  3.21 us (4%)
  between operations  2.68 us (4%)
  local copies, waits for them, and re-layouts  0.8 us (1%)
    pallas_call x2, Pallas kernels, deposit(): pl.pallas_call(functools.partial(kernel, blocks=blocks, shift=shift), gri...  23.3 us
    pallas_call x1, Pallas kernels, body(): pl.pallas_call(functools.partial(update_kernel, blocks=blocks), grid=(ste...  10.5 us
    pallas_call x1, Pallas kernels, body(): pl.pallas_call(functools.partial(grid_kernel, row=row, margin=margin, dea...  9.06 us
    ppermute x1, starting transfers between devices, body(): after = lax.ppermute(up, axes, [(i + 1, i) for i in range(count - 1)])  8.34 us
    ppermute x1, starting transfers between devices, body(): lax.ppermute(leave_down, 'slab', [(i, i + 1) for i in range(slabs - 1)])  7.85 us
    ppermute x3, starting transfers between devices, body(): pieces[k] = lax.ppermute(pieces[k], 'deal', pairs)  4.28 us
    ppermute x1, starting transfers between devices, body(): before = lax.ppermute(down, axes, [(i, i + 1) for i in range(count - 1)])  1.92 us
    ppermute x1, starting transfers between devices, body(): lax.ppermute(leave_up, 'slab', [(i + 1, i) for i in range(slabs - 1)])  1.92 us
  transfers between devices with their start and end apart: 7, of which 1 were waited for; matrix products, arithmetic and copies ran while one was open for 1% of the time, Pallas kernels for 33%

profile of v3, /device:TPU:1, one launch (start us, length us, event | category | flops | bytes accessed | tf_op | source)
XLA Modules:
  0.0 75.2 jit_solution(2134810909777697249)
XLA Ops:
  1.3 1.9 %convert_reduce_fusion.1 = (s32[]{:T(128)}, s32[]{:T(128)}, s32[1024]{0:T(1024)}) fusion(s32[1024]{0:T(1024)} %param.14, s32[]{:T(128)S(6)} %sub.9), kind=kLoop, calls=%fused_computation.1 | loop fusion | flops 7166 | bytes 8204 | tf_op jit(solution)/shard_map/reduce_sum | solution.py:265
  4.5 0.6 pad_add_fusion.1.marks_ref
  5.1 9.0 %deposit_edges.1 = (f32[96,8,128]{2,1,0:T(8,128)}, f32[96,8,128]{2,1,0:T(8,128)}) custom-call(s32[3]{0:T(128)} %pad_add_fusion.1.marks_ref, s32[1024]{0:T(1024)} %get-tuple-element.27.tiles_ref, f32[3,1024,128]{2,1,0:T(8,128)} %bitcast.17, f32[3,1024,128]{2,1,0:T(8,128)} %bitcast.24, f32[9,1024,128]{2,1,0:T(8,128)} %bitcast.21, f32[1024,128]{1,0:T(8,128)} %mass_ref.1, ...), custom_call_target="tpu_custom_call" | custom-call | flops 268435456 | bytes 8912896 | tf_op jit(solution)/shard_map/deposit_edges/pallas_call | solution.py:290
  14.1 8.3 %collective-permute-start.1 = (f32[96,8,128]{2,1,0:T(8,128)}, f32[96,8,128]{2,1,0:T(8,128)S(1)}, u32[]{:S(2)}, u32[]{:S(2)}) collective-permute-start(f32[96,8,128]{2,1,0:T(8,128)} %get-tuple-element.14.up_ref), channel_id=1, source_target_pairs={{1,0},{2,1},{3,2},{4,3},{5,4},{6,5},{7,6},{8,7},{9,8},{10,9},{11,1... | collective-permute-start | bytes 1179656 | tf_op jit(solution)/shard_map/ppermute | solution.py:308
  22.5 1.9 %collective-permute-start = (f32[96,8,128]{2,1,0:T(8,128)}, f32[96,8,128]{2,1,0:T(8,128)S(1)}, u32[]{:S(2)}, u32[]{:S(2)}) collective-permute-start(f32[96,8,128]{2,1,0:T(8,128)} %get-tuple-element.15.down_ref), channel_id=1, source_target_pairs={{0,1},{1,2},{2,3},{3,4},{4,5},{5,6},{6,7},{7,8},{8,9},{9,10},{10,1... | collective-permute-start | bytes 1179656 | tf_op jit(solution)/shard_map/ppermute | solution.py:307
  24.4 14.3 %deposit_middle.1.mid_ref = f32[384,8,128]{2,1,0:T(8,128)} custom-call(s32[3]{0:T(128)} %pad_add_fusion.1.marks_ref, s32[1024]{0:T(1024)} %get-tuple-element.27.tiles_ref, f32[3,1024,128]{2,1,0:T(8,128)} %bitcast.18, f32[3,1024,128]{2,1,0:T(8,128)} %bitcast.25, f32[9,1024,128]{2,1,0:T(8,128)} %bitcast.22, f32[1024,128]{1,0:T(8,128)} %mass_ref.1, ...), custom_call_target="tpu_custom_call" | custom-call | flops 268435456 | bytes 8912896 | tf_op jit(solution)/shard_map/deposit_middle/pallas_call | solution.py:290
  38.7 0.7 pad_add_fusion.ends_ref
  39.4 0.0 collective-permute-done.1.after_ref
  39.4 0.1 collective-permute-done.before_ref
  39.5 0.7 copy-done.1
  40.1 0.1 copy-done.2
  40.3 9.1 %grid_step.1 = (f32[576,8,128]{2,1,0:T(8,128)}, f32[3,16,2048]{2,1,0:T(8,128)}, f32[3,16,2048]{2,1,0:T(8,128)}, f32[3,16,2048]{2,1,0:T(8,128)}, f32[3,16,2048]{2...) custom-call(s32[1024]{0:T(1024)} %get-tuple-element.27.tiles_ref, s32[2,16]{1,0:T(2,128)} %bitcast.26, ...), custom_call_target="tpu_custom_call" | custom-call | tf_op jit(solution)/shard_map/grid_step/pallas_call | solution.py:318
  49.3 3.0 %collective-permute-start.2 = (f32[3,16,2048]{2,1,0:T(8,128)}, f32[3,16,2048]{2,1,0:T(8,128)S(1)}, u32[]{:S(2)}, u32[]{:S(2)}) collective-permute-start(f32[3,16,2048]{2,1,0:T(8,128)} %get-tuple-element.18), channel_id=1, source_target_pairs={{0,1},{1,2},{2,3},{3,0},{4,5},{5,6},{6,7},{7,4},{8,9},{9,10},{10,1... | collective-permute-start | bytes 1179656 | tf_op jit(solution)/shard_map/ppermute | solution.py:331
  52.3 0.0 collective-permute-start.3
  52.3 1.2 %collective-permute-start.4 = (f32[3,16,2048]{2,1,0:T(8,128)}, f32[3,16,2048]{2,1,0:T(8,128)S(1)}, u32[]{:S(2)}, u32[]{:S(2)}) collective-permute-start(f32[3,16,2048]{2,1,0:T(8,128)} %get-tuple-element.20), channel_id=1, source_target_pairs={{0,3},{1,0},{2,1},{3,2},{4,7},{5,4},{6,5},{7,6},{8,11},{9,8},{10,9... | collective-permute-start | bytes 1179656 | tf_op jit(solution)/shard_map/ppermute | solution.py:331
  53.6 7.9 %collective-permute-start.5 = (f32[16,16,128]{2,1,0:T(8,128)}, f32[16,16,128]{2,1,0:T(8,128)S(1)}, u32[]{:S(2)}, u32[]{:S(2)}) collective-permute-start(f32[16,16,128]{2,1,0:T(8,128)} %get-tuple-element.21), channel_id=1, source_target_pairs={{0,4},{4,8},{8,12},{12,16},{16,20},{20,24},{24,28},{1,5},{5,9},{9,... | collective-permute-start | bytes 393224 | tf_op jit(solution)/shard_map/ppermute | solution.py:332
  61.5 1.9 %collective-permute-start.6 = (f32[16,16,128]{2,1,0:T(8,128)}, f32[16,16,128]{2,1,0:T(8,128)S(1)}, u32[]{:S(2)}, u32[]{:S(2)}) collective-permute-start(f32[16,16,128]{2,1,0:T(8,128)} %get-tuple-element.22), channel_id=1, source_target_pairs={{4,0},{8,4},{12,8},{16,12},{20,16},{24,20},{28,24},{5,1},{9,5},{13... | collective-permute-start | bytes 393224 | tf_op jit(solution)/shard_map/ppermute | solution.py:333
  63.4 10.5 %update.1 = f32[15,1024,128]{2,1,0:T(8,128)} custom-call(s32[1024]{0:T(1024)} %get-tuple-element.27.tiles_ref, f32[3,1024,128]{2,1,0:T(8,128)} %bitcast.20, s32[1024,128]{1,0:T(8,128)} %cell_ref.3, f32[576,8,128]{2,1,0:T(8,128)} %get-tuple-element.16.settled_ref), custom_call_target="tpu_custom_call" | custom-call | flops 7864320 | bytes 10485760 | tf_op jit(solution)/shard_map/update/pallas_call | solution.py:335
  73.9 0.0 collective-permute-done.5.refs_4_
  73.9 0.0 collective-permute-done.6.refs_5_
  73.9 0.0 collective-permute-done.2.refs_1_
  73.9 0.0 collective-permute-done.3.refs_2_
  73.9 0.0 collective-permute-done.4.refs_3_
  73.9 1.3 %assemble.1 = (f32[3,64,2048]{2,1,0:T(8,128)}, f32[2,16,16,128]{3,2,1,0:T(8,128)}) custom-call(s32[1]{0:T(128)} %bitcast.5.deal_ref, f32[3,16,2048]{2,1,0:T(8,128)S(1)} %copy-done, f32[3,16,2048]{2,1,0:T(8,128)S(1)} %collective-permute-done.2.refs_1_, f32[3,16,2048]{2,1,0:T(8,128)S(1)} %collective-permute-done.3.refs_2_, ...), custom_call_target="tpu_custom_call" | custom-call | tf_op jit(solution)/shard_map/assemble/pallas_call | solution.py:352
  (4 shorter events, 0.0 us)
Async XLA Ops:
  14.1 25.2 %collective-permute-start.1 = (f32[96,8,128]{2,1,0:T(8,128)}, f32[96,8,128]{2,1,0:T(8,128)S(1)}, u32[]{:S(2)}, u32[]{:S(2)}) collective-permute-start(f32[96,8,128]{2,1,0:T(8,128)} %get-tuple-element.14.up_ref), channel_id=1, source_target_pairs={{1,0},{2,1},{3,2},{4,3},{5,4},{6,5},{7,6},{8,7},{9,8},{10,9},{11,1... | collective-permute-start | bytes 1179656 | tf_op jit(solution)/shard_map/ppermute | solution.py:308
  22.5 17.0 %collective-permute-start = (f32[96,8,128]{2,1,0:T(8,128)}, f32[96,8,128]{2,1,0:T(8,128)S(1)}, u32[]{:S(2)}, u32[]{:S(2)}) collective-permute-start(f32[96,8,128]{2,1,0:T(8,128)} %get-tuple-element.15.down_ref), channel_id=1, source_target_pairs={{0,1},{1,2},{2,3},{3,4},{4,5},{5,6},{6,7},{7,8},{8,9},{9,10},{10,1... | collective-permute-start | bytes 1179656 | tf_op jit(solution)/shard_map/ppermute | solution.py:307
  39.4 0.8 %copy-start.1 = (f32[96,8,128]{2,1,0:T(8,128)}, f32[96,8,128]{2,1,0:T(8,128)S(1)}, u32[]{:S(2)}) copy-start(f32[96,8,128]{2,1,0:T(8,128)S(1)} %collective-permute-done.1.after_ref) | copy-start | bytes 1179652
  39.5 0.8 %copy-start.2 = (f32[96,8,128]{2,1,0:T(8,128)}, f32[96,8,128]{2,1,0:T(8,128)S(1)}, u32[]{:S(2)}) copy-start(f32[96,8,128]{2,1,0:T(8,128)S(1)} %collective-permute-done.before_ref) | copy-start | bytes 1179652
  49.3 24.6 %collective-permute-start.2 = (f32[3,16,2048]{2,1,0:T(8,128)}, f32[3,16,2048]{2,1,0:T(8,128)S(1)}, u32[]{:S(2)}, u32[]{:S(2)}) collective-permute-start(f32[3,16,2048]{2,1,0:T(8,128)} %get-tuple-element.18), channel_id=1, source_target_pairs={{0,1},{1,2},{2,3},{3,0},{4,5},{5,6},{6,7},{7,4},{8,9},{9,10},{10,1... | collective-permute-start | bytes 1179656 | tf_op jit(solution)/shard_map/ppermute | solution.py:331
  52.3 21.6 %collective-permute-start.3 = (f32[3,16,2048]{2,1,0:T(8,128)}, f32[3,16,2048]{2,1,0:T(8,128)S(1)}, u32[]{:S(2)}, u32[]{:S(2)}) collective-permute-start(f32[3,16,2048]{2,1,0:T(8,128)} %get-tuple-element.19), channel_id=1, source_target_pairs={{0,2},{1,3},{2,0},{3,1},{4,6},{5,7},{6,4},{7,5},{8,10},{9,11},{10,... | collective-permute-start | bytes 1179656 | tf_op jit(solution)/shard_map/ppermute | solution.py:331
  52.3 21.6 %collective-permute-start.4 = (f32[3,16,2048]{2,1,0:T(8,128)}, f32[3,16,2048]{2,1,0:T(8,128)S(1)}, u32[]{:S(2)}, u32[]{:S(2)}) collective-permute-start(f32[3,16,2048]{2,1,0:T(8,128)} %get-tuple-element.20), channel_id=1, source_target_pairs={{0,3},{1,0},{2,1},{3,2},{4,7},{5,4},{6,5},{7,6},{8,11},{9,8},{10,9... | collective-permute-start | bytes 1179656 | tf_op jit(solution)/shard_map/ppermute | solution.py:331
  53.6 20.3 %collective-permute-start.5 = (f32[16,16,128]{2,1,0:T(8,128)}, f32[16,16,128]{2,1,0:T(8,128)S(1)}, u32[]{:S(2)}, u32[]{:S(2)}) collective-permute-start(f32[16,16,128]{2,1,0:T(8,128)} %get-tuple-element.21), channel_id=1, source_target_pairs={{0,4},{4,8},{8,12},{12,16},{16,20},{20,24},{24,28},{1,5},{5,9},{9,... | collective-permute-start | bytes 393224 | tf_op jit(solution)/shard_map/ppermute | solution.py:332
  61.5 12.4 %collective-permute-start.6 = (f32[16,16,128]{2,1,0:T(8,128)}, f32[16,16,128]{2,1,0:T(8,128)S(1)}, u32[]{:S(2)}, u32[]{:S(2)}) collective-permute-start(f32[16,16,128]{2,1,0:T(8,128)} %get-tuple-element.22), channel_id=1, source_target_pairs={{4,0},{8,4},{12,8},{16,12},{20,16},{24,20},{28,24},{5,1},{9,5},{13... | collective-permute-start | bytes 393224 | tf_op jit(solution)/shard_map/ppermute | solution.py:333
  63.4 10.5 %copy-start = (f32[3,16,2048]{2,1,0:T(8,128)S(1)}, f32[3,16,2048]{2,1,0:T(8,128)}, u32[]{:S(2)}) copy-start(f32[3,16,2048]{2,1,0:T(8,128)} %get-tuple-element.17.refs_0_) | copy-start | bytes 1179652
